TPU v7x, 128 devices: a whole 4x4x4 slice. The times are simulated.
128 devices in a mesh: row: 16 (over y, z), col: 8 (over x, core).
Axes of the slice: x: 4, y: 4, z: 4, core: 2. Of those that a mesh axis runs over, the one named last changes fastest.
Arguments:
- covariance: float32 [2, 16, 512, 4, 8, 512], P(None, 'row', None, None, 'col'), as said below
- noise_var: float32 [2, 16, 512], P(None, 'row'), may hold values from 0.3 to 1.5
- observed: float32 [2, 16, 512, 1024], P(None, 'row', None, 'col'), may hold values from -6 to 6
- cloud_free: int32 [2, 16, 512, 1024], P(None, 'row', None, 'col'), may hold values 0 or 1
Outputs:
- factor: float32 [2, 16, 512, 4, 8, 512], P(None, 'row', None, None, 'col')
- reduced: float32 [2, 16, 512, 1024], P(None, 'row', None, 'col')
Inputs may be any that keep to these rules, and one draw needn't show every extreme that they name: covariance is symmetric and v^T covariance v >= 0.25 v^T v for every vector v.
All inputs are finite; a program needn't handle non-finite values. No bound on the sum of `cloud_free` on one device may be relied on, other than what follows from the above.
Results may differ from a plain program's by a relative error of at most 0.00024.
Values sent between devices are 32-bit elements; how exact they have to be, the bound alone decides.
A program may use at most 128 MiB of HBM per device.

v0:
```python
import jax
import jax.numpy as jnp
from jax import lax
from jax.sharding import PartitionSpec as P

PANELS = 2


HIGHEST = lax.Precision.HIGHEST


def broadcast(block, axis, owner):
    block = jnp.where(lax.axis_index(axis) == owner, block, jnp.zeros_like(block))
    return lax.psum(block, axis)


def place_panel(solved, corner, row_global, section):
    return jnp.where(
        row_global[:, None, None] > section,
        solved,
        jnp.where(row_global[:, None, None] == section, corner[None], 0.0),
    )


def body(covariance, noise_var, observed, cloud_free):
    row_count = lax.axis_size("row")
    col_count = lax.axis_size("col")
    row_index = lax.axis_index("row")
    column_index = lax.axis_index("col")
    local_rows = covariance.shape[0]
    panel_width = covariance.shape[2]
    local_cols = covariance.shape[3]
    series = observed.shape[3]
    matrix = covariance.reshape(local_rows, panel_width, local_cols, panel_width)
    noise_local = noise_var.reshape(local_rows, panel_width)
    targets = (observed * cloud_free.astype(jnp.float32)).reshape(local_rows, panel_width, series)
    row_global = jnp.arange(local_rows, dtype=jnp.int32) * row_count + row_index
    column_global = jnp.arange(local_cols, dtype=jnp.int32) * col_count + column_index
    identity = jnp.eye(panel_width, dtype=jnp.float32)
    on_diagonal = (row_global[:, None] == column_global[None, :]).astype(jnp.float32)
    matrix = matrix + on_diagonal[:, None, :, None] * (
        noise_local[:, :, None, None] * identity[None, :, None, :]
    )
    repeat_count = row_count // col_count
    for section in range(PANELS):
        row_root = section % row_count
        row_slot = section // row_count
        column_root = section % col_count
        column_slot = section // col_count
        owner_here = jnp.logical_and(row_index == row_root, column_index == column_root)
        diag_block = jnp.where(owner_here, matrix[row_slot, :, column_slot, :], identity)
        factor_local = jnp.linalg.cholesky(diag_block)
        column = matrix[:, :, column_slot, :].reshape(local_rows * panel_width, panel_width)
        corner = broadcast(factor_local, "row", row_root)
        solved = lax.linalg.triangular_solve(
            corner, column, left_side=False, lower=True, transpose_a=True
        )
        blocks = place_panel(
            solved.reshape(local_rows, panel_width, panel_width), corner, row_global, section
        )
        blocks = broadcast(blocks, "col", column_root)
        pieces = []
        for repeat in range(repeat_count):
            pieces.append(broadcast(blocks, "row", column_index + repeat * col_count))
        across = jnp.stack(pieces, axis=1).reshape(local_cols, panel_width, panel_width)
        left_masked = jnp.where(row_global[:, None, None] > section, blocks, 0.0)
        right_masked = jnp.where(column_global[:, None, None] > section, across, 0.0)
        matrix = matrix - jnp.einsum("aik,cjk->aicj", left_masked, right_masked, precision=HIGHEST)
        matrix = matrix.at[:, :, column_slot, :].set(
            jnp.where(column_index == column_root, blocks, matrix[:, :, column_slot, :])
        )
        lead_block = jnp.where(row_index == row_root, blocks[row_slot], identity)
        head_solve = lax.linalg.triangular_solve(
            lead_block, targets[row_slot], left_side=True, lower=True
        )
        head_solve = broadcast(head_solve, "row", row_root)
        below_update = jnp.einsum("aik,kj->aij", blocks, head_solve, precision=HIGHEST)
        targets = jnp.where(
            row_global[:, None, None] > section,
            targets - below_update,
            jnp.where(row_global[:, None, None] == section, head_solve[None], targets),
        )
    upper_zero = jnp.logical_and(
        row_global[:, None, None, None] < PANELS, column_global[None, None, :, None] >= PANELS
    )
    matrix = jnp.where(upper_zero, 0.0, matrix)
    return (
        matrix.reshape(local_rows, 1, panel_width, local_cols, 1, panel_width),
        targets.reshape(local_rows, 1, panel_width, series),
    )


def solution(mesh):
    placed = (
        P(None, "row", None, None, "col", None),
        P(None, "row", None),
        P(None, "row", None, "col"),
        P(None, "row", None, "col"),
    )
    return jax.shard_map(
        body,
        mesh=mesh,
        in_specs=placed,
        out_specs=(P(None, "row", None, None, "col", None), P(None, "row", None, "col")),
        check_vma=False,
    )
```

profile of v0, /device:TPU:18, one launch (start us, length us, event | category | flops | bytes accessed | tf_op | source)
XLA Modules:
  0.0 1056.2 jit_solution(14155982489307563679)
XLA Ops:
  7.4 20.6 %copy.37 = f32[2,1,512,4,1,512]{2,5,0,3,4,1:T(8,128)} copy(f32[2,1,512,4,1,512]{5,4,3,2,1,0:T(1,128)} %param.13) | data formatting | bytes 16777216 | tf_op args[0]
  38.5 11.7 %cholesky.286 = f32[128,128]{1,0:T(8,128)S(1)} custom-call(f32[128,128]{1,0:T(8,128)S(1)} %cholesky.426), custom_call_target="Cholesky" | custom-call | tf_op jit(solution)/shard_map/jit(cholesky)/cholesky | solution.py:52
  61.0 12.0 %cholesky.305 = f32[128,128]{1,0:T(8,128)S(1)} custom-call(f32[128,128]{1,0:T(8,128)S(1)} %cholesky.430), custom_call_target="Cholesky" | custom-call | tf_op jit(solution)/shard_map/jit(cholesky)/cholesky | solution.py:52
  84.0 11.7 %cholesky.326 = f32[128,128]{1,0:T(8,128)S(1)} custom-call(f32[128,128]{1,0:T(8,128)S(1)} %cholesky.435), custom_call_target="Cholesky" | custom-call | tf_op jit(solution)/shard_map/jit(cholesky)/cholesky | solution.py:52
  106.5 21.9 %cholesky.343 = f32[128,128]{1,0:T(8,128)S(1)} custom-call(f32[128,128]{1,0:T(8,128)S(1)} %convolution_subtract_fusion.17), custom_call_target="Cholesky" | custom-call | tf_op jit(solution)/shard_map/jit(cholesky)/cholesky | solution.py:52
  137.7 84.8 %all-reduce.11.cloned.1.call-done = f32[512,512]{0,1:T(8,128)} async-done(((f32[512,512]{0,1:T(8,128)}), f32[512,512]{0,1:T(8,128)}) %all-reduce.11.cloned.1.call-update) | async-done | bytes 1048592 | tf_op jit(solution)/shard_map/psum | solution.py:14
  233.2 40.1 %custom-call.34 = f32[4,128,128]{1,2,0:T(8,128)S(1)} custom-call(f32[4,128,128]{2,1,0:T(8,128)} %copy-done.17), custom_call_target="InvertDiagBlocksLowerTriangular" | custom-call | tf_op jit(solution)/shard_map/triangular_solve/custom-call.3 | solution.py:55
  287.9 63.2 %all-reduce.13.cloned.1.call-done = f32[2,512,512]{1,2,0:T(8,128)} async-done(((f32[2,512,512]{1,2,0:T(8,128)}), f32[2,512,512]{1,2,0:T(8,128)}) %all-reduce.13.cloned.1.call-update) | async-done | bytes 2097168 | tf_op jit(solution)/shard_map/psum | solution.py:14
  358.8 12.4 %while.12 = (s32[]{:T(128)}, f32[512,512]{0,1:T(8,128)}, s32[4,2]{0,1:T(2,128)S(1)}, f32[4,128,128]{2,1,0:T(8,128)S(1)}, s32[]{:T(128)}) while((s32[]{:T(128)}, f32[512,512]{0,1:T(8,128)}, s32[4,2]{0,1:T(2,128)S(1)}, f32[4,128,128]{2,1,0:T(8,128)S(1)}, s32[]{:T(128)}) %tuple.126), condition=%wide.while_cond.3, body=%wide.while_body.3.sunk | while | flops 2 | bytes 393329 | solution.py:73
  371.1 39.3 %custom-call.39 = f32[4,128,128]{1,2,0:T(8,128)S(1)} custom-call(f32[4,128,128]{2,1,0:T(8,128)S(1)} %get-tuple-element.59), custom_call_target="InvertDiagBlocksLowerTriangular" | custom-call | tf_op jit(solution)/shard_map/triangular_solve/custom-call.8 | solution.py:73
  416.2 45.4 %all-reduce.21.cloned.1.call-done = (f32[2,1,512,512]{2,3,0,1:T(8,128)}, f32[2,1,512,512]{2,3,0,1:T(8,128)}) async-done(((f32[2,1,512,512]{2,3,0,1:T(8,128)}, f32[2,1,512,512]{2,3,0,1:T(8,128)}), (f32[2,1,512,512]{2,3,0,1:T(8,128)}, f32[2,1,512,512]{2,3,0,1:T(8,128)})) %all-reduce.21.cloned.1.call-update) | async-done | bytes 4194320 | tf_op jit(solution)/shard_map/psum | solution.py:14
  474.2 18.3 %fusion.4 = f32[2,512,4,512]{1,3,0,2:T(8,128)S(1)} fusion(f32[2,512,4,512]{1,3,0,2:T(8,128)} %copy-done, f32[4,512,512]{2,1,0:T(8,128)S(1)} %bitcast_select_fusion.1, f32[2,512,512]{1,2,0:T(8,128)S(1)} %copy-done.2, pred[2]{0:T(512)(128)(4,1)S(1)} %get-tuple-element.163), kind=kOutput, calls=%fused_computation.18 | convolution fusion | flops 12887523328 | bytes 23068674 | tf_op jit(solution)/shard_map/aik,cjk->aicj/dot_general | solution.py:68
  501.0 11.7 %cholesky.358 = f32[128,128]{1,0:T(8,128)S(1)} custom-call(f32[128,128]{1,0:T(8,128)S(1)} %cholesky.439), custom_call_target="Cholesky" | custom-call | tf_op jit(solution)/shard_map/jit(cholesky)/cholesky | solution.py:52
  524.7 11.7 %cholesky.377 = f32[128,128]{1,0:T(8,128)S(1)} custom-call(f32[128,128]{1,0:T(8,128)S(1)} %cholesky.443), custom_call_target="Cholesky" | custom-call | tf_op jit(solution)/shard_map/jit(cholesky)/cholesky | solution.py:52
  551.1 11.7 %cholesky.398 = f32[128,128]{1,0:T(8,128)S(1)} custom-call(f32[128,128]{1,0:T(8,128)S(1)} %cholesky.448), custom_call_target="Cholesky" | custom-call | tf_op jit(solution)/shard_map/jit(cholesky)/cholesky | solution.py:52
  574.4 11.9 %cholesky.415 = f32[128,128]{1,0:T(8,128)S(1)} custom-call(f32[128,128]{1,0:T(8,128)S(1)} %convolution_subtract_fusion.16), custom_call_target="Cholesky" | custom-call | tf_op jit(solution)/shard_map/jit(cholesky)/cholesky | solution.py:52
  596.0 83.1 %all-reduce.19.cloned.1.call-done = (f32[512,512]{0,1:T(8,128)}, f32[512,128]{1,0:T(8,128)}) async-done(((f32[512,512]{0,1:T(8,128)}, f32[512,128]{1,0:T(8,128)}), (f32[512,512]{0,1:T(8,128)}, f32[512,128]{1,0:T(8,128)})) %all-reduce.19.cloned.1.call-update) | async-done | bytes 1310736 | tf_op jit(solution)/shard_map/psum | solution.py:14
  689.9 40.1 %custom-call.38 = f32[4,128,128]{1,2,0:T(8,128)S(1)} custom-call(f32[4,128,128]{2,1,0:T(8,128)} %copy-done.18), custom_call_target="InvertDiagBlocksLowerTriangular" | custom-call | tf_op jit(solution)/shard_map/triangular_solve/custom-call.3 | solution.py:55
  755.8 59.3 %all-reduce.15.cloned.1.call-done = f32[2,512,512]{1,2,0:T(8,128)} async-done(((f32[2,512,512]{1,2,0:T(8,128)}), f32[2,512,512]{1,2,0:T(8,128)}) %all-reduce.15.cloned.1.call-update) | async-done | bytes 2097168 | tf_op jit(solution)/shard_map/psum | solution.py:14
  817.5 12.5 %while.13 = (s32[]{:T(128)}, f32[512,512]{0,1:T(8,128)}, s32[4,2]{0,1:T(2,128)S(1)}, f32[4,128,128]{2,1,0:T(8,128)S(1)}, s32[]{:T(128)}) while((s32[]{:T(128)}, f32[512,512]{0,1:T(8,128)}, s32[4,2]{0,1:T(2,128)S(1)}, f32[4,128,128]{2,1,0:T(8,128)S(1)}, s32[]{:T(128)}) %tuple.128), condition=%wide.while_cond.3.clone, body=%wide.while_body.3.clone.sunk | while | flops 2 | bytes 393329 | solution.py:73
  830.7 40.1 %custom-call.40 = f32[4,128,128]{1,2,0:T(8,128)S(1)} custom-call(f32[4,128,128]{2,1,0:T(8,128)} %copy-done.16), custom_call_target="InvertDiagBlocksLowerTriangular" | custom-call | tf_op jit(solution)/shard_map/triangular_solve/custom-call.8 | solution.py:73
  882.6 105.4 %all-reduce.17.cloned.1.call-done = (f32[2,1,512,512]{2,3,0,1:T(8,128)}, f32[2,1,512,512]{2,3,0,1:T(8,128)}, f32[512,128]{1,0:T(8,128)}) async-done(((f32[2,1,512,512]{2,3,0,1:T(8,128)}, f32[2,1,512,512]{2,3,0,1:T(8,128)}, f32[512,128]{1,0:T(8,128)}), (f32[2,1,512,512]{2,3,0,1:T(8,128)}, f32[2,1,512,512]{2,3,0,1:T(8,128)}, f32[512,128]{1,0:T(8,128)})) %all-reduce.17.cloned.1.call-update) | async-done | bytes 4456464 | tf_op jit(solution)/shard_map/psum | solution.py:14
  1000.6 18.3 %fusion.7 = f32[2,512,4,512]{1,3,0,2:T(8,128)S(1)} fusion(f32[2,512,4,512]{1,3,0,2:T(8,128)} %bitcast_dynamic-update-slice_fusion.4, f32[4,512,512]{2,1,0:T(8,128)S(1)} %bitcast_select_fusion, f32[2,512,512]{1,2,0:T(8,128)S(1)} %copy-done.3, pred[2]{0:T(512)(128)(4,1)S(1)} %get-tuple-element.161), kind=kOutput, calls=%fused_computation.19 | convolution fusion | flops 12887523328 | bytes 23068674 | tf_op jit(solution)/shard_map/aik,cjk->aicj/dot_general | solution.py:68
  1023.8 20.8 %copy.74 = f32[2,1,512,4,1,512]{5,4,3,2,1,0:T(1,128)} copy(f32[2,1,512,4,1,512]{2,5,0,3,4,1:T(8,128)} %select_bitcast_fusion) | data formatting | bytes 16777216
  (288 shorter events, 269.2 us)
Async XLA Ops:
  7.2 215.3 %all-reduce.11.cloned.1.call-start = ((), (), s32[]{:S(2)}) async-start(), calls=%async_computation | async-start | bytes 2097152 | tf_op jit(solution)/shard_map/psum | solution.py:14
  7.4 20.6 %copy-start.19 = (f32[2,1,512]{2,1,0:T(1,128)S(1)}, f32[2,1,512]{2,1,0:T(1,128)}, u32[]{:S(2)}) copy-start(f32[2,1,512]{2,1,0:T(1,128)} %param.14) | copy-start | bytes 12292
  33.2 3.4 copy-start
  134.2 1.6 slice-start
  134.2 216.9 %all-reduce.13.cloned.1.call-start = ((), (), s32[]{:S(2)}) async-start(), calls=%async_computation.1 | async-start | bytes 4194304 | tf_op jit(solution)/shard_map/psum | solution.py:14
  137.7 135.7 %copy-start.5 = (f32[2,512,1,512]{3,1,0,2:T(8,128)S(1)}, f32[2,512,1,512]{3,1,0,2:T(8,128)}, u32[]{:S(2)}) copy-start(f32[2,512,1,512]{3,1,0,2:T(8,128)} %copy.47) | copy-start | bytes 6291460
  283.6 2.0 copy-start.8
  287.4 174.2 %all-reduce.21.cloned.1.call-start = ((), (), s32[]{:S(2)}) async-start(), calls=%async_computation.5 | async-start | bytes 8388608 | tf_op jit(solution)/shard_map/psum | solution.py:14
  355.3 1.0 copy-start.13
  355.3 2.2 copy-start.2
  355.4 323.8 %all-reduce.19.cloned.1.call-start = ((), (), s32[]{:S(2)}) async-start(), calls=%async_computation.4 | async-start | bytes 2621440 | tf_op jit(solution)/shard_map/psum | solution.py:14
  357.5 1.3 copy-start.9
  492.5 3.4 copy-start.1
  496.4 1.3 copy-start.4
  501.0 36.2 %copy-start.11 = (f32[512,512]{1,0:T(8,128)}, f32[512,512]{1,0:T(8,128)S(1)}, u32[]{:S(2)}) copy-start(f32[512,512]{1,0:T(8,128)S(1)} %fusion.47) | copy-start | bytes 3145732
  548.3 38.7 %copy-start.21 = (f32[128]{0:T(128)S(1)}, f32[128]{0:T(128)}, u32[]{:S(2)}) copy-start(f32[128]{0:T(128)} %get-tuple-element.150) | copy-start | bytes 1540
  592.6 222.6 %all-reduce.15.cloned.1.call-start = ((), (), s32[]{:S(2)}) async-start(), calls=%async_computation.2 | async-start | bytes 4194304 | tf_op jit(solution)/shard_map/psum | solution.py:14
  730.0 4.5 copy-start.6
  744.9 3.0 copy-start.7
  744.9 3.0 copy-start.20
  751.3 1.1 copy-start.14
  751.3 236.7 %all-reduce.17.cloned.1.call-start = ((), (), s32[]{:S(2)}) async-start(), calls=%async_computation.3 | async-start | bytes 8912896 | tf_op jit(solution)/shard_map/psum | solution.py:14
  817.5 59.1 %copy-start.3 = (f32[2,512,512]{1,2,0:T(8,128)S(1)}, f32[2,512,512]{1,2,0:T(8,128)}, u32[]{:S(2)}) copy-start(f32[2,512,512]{1,2,0:T(8,128)} %all-reduce.15.cloned.1.call-done) | copy-start | bytes 6291460
  1023.8 20.8 %copy-start.15 = (f32[512,128]{1,0:T(8,128)S(1)}, f32[512,128]{1,0:T(8,128)}, u32[]{:S(2)}) copy-start(f32[512,128]{1,0:T(8,128)} %get-tuple-element.131) | copy-start | bytes 786436
  (5 other events, 3.8 us)
Sparse Core Ops, SparseCore 0:
  134.3 88.0 all-reduce.10
  287.5 63.5 all-reduce.12
  355.5 106.0 all-reduce.20
  592.7 86.4 all-reduce.18
  751.4 63.7 all-reduce.14
  879.5 108.3 all-reduce.16
where the time goes:
time: 1070 us; the launch traced here: 1060 us
  waiting for transfers between devices  441 us (41%)
  other arithmetic  383 us (36%)
  local copies, waits for them, and re-layouts  130 us (12%)
  matrix products  80 us (7%)
  between operations  20.6 us (2%)
    psum x6, waiting for transfers between devices, broadcast(): return lax.psum(block, axis)  441 us
    another operation x29, other arithmetic, body(): factor_local = jnp.linalg.cholesky(diag_block)  169 us
    another operation x7, other arithmetic, body(): lax.linalg.triangular_solve(corner, column, left_side=False, lower=True,...  84.6 us
    another operation x4, other arithmetic, body(): lax.linalg.triangular_solve(lead_block, targets[row_slot], left_side=True...  82.9 us
    unnamed x47, local copies, waits for them, and re-layouts  54.1 us
    dot_general x2, matrix products, body(): jnp.einsum('aik,cjk->aicj', left_masked, right_masked, precision=HIGHEST)  36.6 us
    another operation x40, local copies, waits for them, and re-layouts, body(): lax.linalg.triangular_solve(lead_block, targets[row_slot], left_side=True...  24.6 us
    another operation x47, local copies, waits for them, and re-layouts, body(): lax.linalg.triangular_solve(corner, column, left_side=False, lower=True,...  21.8 us
  transfers between devices with their start and end apart: 6, of which 6 were waited for; matrix products, arithmetic and copies ran while one was open for 7% of the time, Pallas kernels for 0%

commit v1 on v0

v1 whole, which is shorter than its diff:
```python
import jax
import jax.numpy as jnp
from jax import lax
from jax.experimental import pallas as pl
from jax.experimental.pallas import tpu as pltpu
from jax.sharding import PartitionSpec as P

MESH = pl.DeviceIdType.MESH
HIGHEST = lax.Precision.HIGHEST
HIGH = lax.Precision.HIGH
PW = 512
NB = 2 * PW
BK = 128
CH = 32
GC = 128

TREES = (
    (1, 11, 9, 0, 0, 7, 1, 0, 0, 4, 1, 0, 0, 4, 9, 0),
    (2, 0, 0, 0, 7, 8, 8, 14, 3, 3, 2, 2, 0, 0, 0, 0),
    (4, 0, 6, 14, 0, 0, 6, 1, 0, 0, 4, 1, 0, 0, 4, 13),
    (8, 0, 0, 0, 0, 0, 0, 0, 12, 8, 8, 12, 13, 11, 2, 2),
)


def spread_kernel(hsrc, gsrc, H, G, K, hr, hs, kr, ks, gr, gs):
    width = hsrc.shape[1]
    row, col = lax.axis_index("row"), lax.axis_index("col")
    y, z, x, core = row // 4, row % 4, col // 2, col % 2
    where = [
        (y * 4 + (z + 1) % 4, col),
        (((y + 1) % 4) * 4 + z, col),
        (y * 4 + (z + 3) % 4, col),
        (((y + 3) % 4) * 4 + z, col),
        (row, ((x + 1) % 4) * 2 + core),
        (row, ((x + 3) % 4) * 2 + core),
        (row, x * 2 + 1 - core),
    ]
    barrier = pltpu.get_barrier_semaphore()
    for device in where:
        pl.semaphore_signal(barrier, inc=1, device_id=device, device_id_type=MESH)
    pl.semaphore_wait(barrier, len(where))

    masks = []
    for root in range(2):
        place = y * 4 + (z + 4 - root) % 4
        per = []
        for tree in TREES:
            m = jnp.int32(0)
            for at, bits in enumerate(tree):
                if bits:
                    m = jnp.where(place == at, bits, m)
            per.append(m)
        masks.append(per)

    def hslice(ref, root, part, c):
        rows = pl.ds(c * CH, CH)
        cols = pl.ds(0, PW) if part == 0 else pl.ds(PW, width - PW)
        return ref.at[rows, cols] if root is None else ref.at[root, rows, cols]

    def kslice(block, c):
        return K.at[block, pl.ds(c * CH, CH), :]

    def gslice(half, g):
        return G.at[half, pl.ds(g * GC, GC), :]

    def remote(ref, send, recv, device):
        return pltpu.make_async_remote_copy(
            src_ref=ref, dst_ref=ref, send_sem=send, recv_sem=recv, device_id=device, device_id_type=MESH
        )

    for root in range(2):

        @pl.when(row == root)
        def _():
            for part in range(2):
                for c in range(16):
                    pltpu.make_async_copy(
                        hslice(hsrc, None, part, c), hslice(H, root, part, c), hr.at[root, part, c]
                    ).start()

    for half in range(2):

        @pl.when(col == half)
        def _():
            for g in range(8):
                pltpu.make_async_copy(gsrc.at[pl.ds(g * GC, GC), :], gslice(half, g), gr.at[half, g]).start()

    ends = []

    def send(cond, ref, ssem, recv, device):
        copy = remote(ref, ssem, recv, device)

        @pl.when(cond)
        def _():
            copy.start()

        ends.append((cond, copy))

    def h_step(root, part, c):
        ref = hslice(H, root, part, c)
        recv = hr.at[root, part, c]
        remote(ref, hs.at[root, part, c, 0], recv, where[0]).wait_recv()
        tree = c % 4
        for d in range(4):
            if any(bits >> d & 1 for bits in TREES[tree]):
                cond = (masks[root][tree] >> d) & 1 == 1
                send(cond, ref, hs.at[root, part, c, d], recv, where[d])
        if part == 0:
            for owner_core in range(2):
                if root == 1 and owner_core == 0:
                    continue
                block = root + owner_core

                @pl.when(col == owner_core)
                def _():
                    pltpu.make_async_copy(ref, kslice(block, c), kr.at[block, c]).start()

    def k_step(block, c, sibling):
        carrier = core == min(block, 1)
        ref, recv = kslice(block, c), kr.at[block, c]
        copy = remote(ref, ks.at[block, c, 0], recv, where[6])
        if sibling:

            @pl.when(jnp.logical_not(carrier))
            def _():
                copy.wait_recv()

            return

        @pl.when(carrier)
        def _():
            copy.wait_recv()

        along(carrier, ref, ks.at[block, c], recv, c % 2)

    def along(carrier, ref, sems, recv, way):
        goes = (x != 3) if way == 0 else (x != 1)
        send(jnp.logical_and(carrier, goes), ref, sems.at[0], recv, where[4 + way])
        send(carrier, ref, sems.at[1], recv, where[6])

    def g_step(half, g, sibling):
        carrier = core == half
        ref, recv = gslice(half, g), gr.at[half, g]
        copy = remote(ref, gs.at[half, g, 0], recv, where[6])
        if sibling:

            @pl.when(jnp.logical_not(carrier))
            def _():
                copy.wait_recv()

            return

        @pl.when(carrier)
        def _():
            copy.wait_recv()

        along(carrier, ref, gs.at[half, g], recv, g % 2)

    for n in range(20):
        if n < 16:
            root, part, seq = n // 4 % 2, n // 8, n % 4
            for tree in range(4):
                h_step(root, part, seq * 4 + tree)
        if 1 <= n < 9:
            root, seq = (n - 1) // 4, (n - 1) % 4
            for tree in range(4):
                for block in ((0, 1) if root == 0 else (2,)):
                    k_step(block, seq * 4 + tree, False)
        if 4 <= n < 20 and n % 2 == 0:
            for half in range(2):
                g_step(half, (n - 4) // 2, False)
    for block in range(3):
        for c in range(16):
            k_step(block, c, True)
    for half in range(2):
        for g in range(8):
            g_step(half, g, True)
    for cond, copy in ends:

        @pl.when(cond)
        def _():
            copy.wait_send()


def spread(hsrc, gsrc):
    width = hsrc.shape[1]
    dma = pltpu.SemaphoreType.DMA
    return pl.pallas_call(
        spread_kernel,
        out_shape=(
            jax.ShapeDtypeStruct((2, PW, width), jnp.float32),
            jax.ShapeDtypeStruct((2, NB, PW), jnp.float32),
            jax.ShapeDtypeStruct((3, PW, PW), jnp.float32),
        ),
        in_specs=[pl.BlockSpec(memory_space=pl.ANY)] * 2,
        out_specs=[pl.BlockSpec(memory_space=pl.ANY)] * 3,
        scratch_shapes=[
            dma((2, 2, 16)),
            dma((2, 2, 16, 4)),
            dma((3, 16)),
            dma((3, 16, 2)),
            dma((2, 8)),
            dma((2, 8, 2)),
        ],
        compiler_params=pltpu.CompilerParams(collective_id=0, has_side_effects=True),
    )(hsrc, gsrc)


def dot(a, b, dims=((1,), (0,))):
    return lax.dot_general(a, b, (dims, ((), ())), precision=HIGHEST, preferred_element_type=jnp.float32)


def recip(d):
    r = pltpu.reciprocal(d, approx=True)
    return r * (2.0 - d * r)


def factor128(read):
    lane = lax.broadcasted_iota(jnp.int32, (8, BK), 1)
    sub = lax.broadcasted_iota(jnp.int32, (8, BK), 0)
    R = [read(p) for p in range(16)]
    Q = [jnp.where(lane == sub + 8 * p, 1.0, 0.0) for p in range(16)]
    splat = lambda v: jnp.broadcast_to(v, (8, BK))
    U, W = [], []
    for p in range(16):
        B = [splat(R[p][:, 8 * p + k : 8 * p + k + 1]) for k in range(8)]
        below = {i: [splat(R[i][:, 8 * p + k : 8 * p + k + 1]) for k in range(8)] for i in range(p + 1, 16)}
        Rp, Qp = R[p], Q[p]
        pivots = None
        for j in range(8):
            d = splat(B[j][j : j + 1, :])
            inv = recip(d)
            pivots = d if pivots is None else jnp.where(sub == j, d, pivots)
            coef = jnp.where(sub > j, B[j] * inv, 0.0)
            ur, qr = splat(Rp[j : j + 1, :]), splat(Qp[j : j + 1, :])
            lead = {k: splat(B[k][j : j + 1, :]) for k in range(j + 1, 8)}
            for i in range(p + 1, 16):
                ci = below[i][j] * inv
                for k in range(j + 1, 8):
                    below[i][k] = below[i][k] - ci * lead[k]
                R[i] = R[i] - ci * ur
                Q[i] = Q[i] - ci * qr
            if j < 7:
                for k in range(j + 1, 8):
                    B[k] = B[k] - coef * lead[k]
                Rp = Rp - coef * ur
                Qp = Qp - coef * qr
        scale = lax.rsqrt(pivots)
        U.append(jnp.where(lane >= sub + 8 * p, Rp * scale, 0.0))
        W.append(Qp * scale)
    return U, W


def corner_kernel(k_ref, w_ref, E, D):
    count = NB // BK
    E[0:PW, 0:PW] = k_ref[0]
    E[0:PW, PW:NB] = k_ref[1]
    E[PW:NB, PW:NB] = k_ref[2]
    E[PW:NB, 0:PW] = jnp.zeros((PW, PW), jnp.float32)

    def step(k, carry):
        r0 = pl.multiple_of(k * BK, BK)
        U, W = factor128(lambda p: E[pl.ds(r0 + 8 * p, 8), pl.ds(r0, BK)])
        for p in range(16):
            D[pl.ds(8 * p, 8), :] = W[p]
        E[pl.ds(r0, BK), :] = dot(D[...], E[pl.ds(r0, BK), :])
        E[pl.ds(r0, BK), pl.ds(r0, BK)] = D[...]
        lane = lax.broadcasted_iota(jnp.int32, (BK, NB), 1)
        w_ref[pl.ds(r0, BK), :] = jnp.where(lane < r0 + BK, E[pl.ds(r0, BK), :], 0.0)

        def under(i, carry):
            i0 = pl.multiple_of(i * BK, BK)
            E[pl.ds(i0, BK), pl.ds(r0, BK)] = jnp.zeros((BK, BK), jnp.float32)
            E[pl.ds(i0, BK), :] = E[pl.ds(i0, BK), :] - dot(
                E[pl.ds(r0, BK), pl.ds(i0, BK)], E[pl.ds(r0, BK), :], ((0,), (0,))
            )
            return carry

        lax.fori_loop(k + 1, count, under, 0)
        return carry

    lax.fori_loop(0, count, step, 0)


def corner(blocks):
    return pl.pallas_call(
        corner_kernel,
        out_shape=jax.ShapeDtypeStruct((NB, NB), jnp.float32),
        scratch_shapes=[pltpu.VMEM((NB, NB), jnp.float32), pltpu.VMEM((BK, BK), jnp.float32)],
        compiler_params=pltpu.CompilerParams(vmem_limit_bytes=40 * 2**20),
    )(blocks)


def body(covariance, noise_var, observed, cloud_free):
    row, col = lax.axis_index("row"), lax.axis_index("col")
    series = observed.shape[3]
    matrix = covariance.reshape(2, PW, 4, PW)
    noise = noise_var.reshape(2, PW)
    targets = (observed * cloud_free.astype(jnp.float32)).reshape(2, PW, series)
    rows = jnp.arange(2, dtype=jnp.int32) * 16 + row
    cols = jnp.arange(4, dtype=jnp.int32) * 8 + col
    same = (rows[:, None] == cols[None, :])[:, None, :, None]
    eye = jnp.eye(PW, dtype=bool)[None, :, None, :]
    matrix = matrix + jnp.where(jnp.logical_and(same, eye), noise[:, :, None, None], 0.0)
    wide = matrix.reshape(NB, 4 * PW)
    hsrc = jnp.concatenate([wide[:PW], targets[0]], axis=1)
    H, G, K = spread(hsrc, wide[:, :PW])
    W = corner(K)
    H = H.reshape(NB, 4 * PW + series)
    left = jnp.concatenate([G[0], G[1]], axis=1)
    X = lax.dot_general(left, W, (((1,), (1,)), ((), ())), precision=HIGH)
    T = jnp.dot(X, W, precision=HIGH)
    full = jnp.concatenate([wide, targets.reshape(NB, series)], axis=1) - jnp.dot(T, H, precision=HIGH)
    head = jnp.dot(W, H[:, 4 * PW :], precision=HIGH).reshape(2, PW, series)
    reduced = full[:, 4 * PW :].reshape(2, PW, series)
    head_here = jnp.where(row == 0, head[0], head[1])
    first = jnp.where(row < 2, head_here, reduced[0])
    reduced = jnp.stack([first, reduced[1]])
    panel = jnp.where(col == 0, X[:, :PW], X[:, PW:])
    r_at = (rows[:, None] * PW + jnp.arange(PW, dtype=jnp.int32)[None, :]).reshape(NB)
    c_at = col * PW + jnp.arange(PW, dtype=jnp.int32)
    panel = jnp.where(r_at[:, None] >= c_at[None, :], panel, 0.0)
    rest = jnp.where(r_at[:, None] < NB, 0.0, full[:, : 4 * PW])
    factor = jnp.concatenate([jnp.where(col < 2, panel, rest[:, :PW]), rest[:, PW:]], axis=1)
    return factor.reshape(covariance.shape), reduced.reshape(observed.shape)


def solution(mesh):
    placed = (
        P(None, "row", None, None, "col", None),
        P(None, "row", None),
        P(None, "row", None, "col"),
        P(None, "row", None, "col"),
    )
    return jax.shard_map(
        body,
        mesh=mesh,
        in_specs=placed,
        out_specs=(P(None, "row", None, None, "col", None), P(None, "row", None, "col")),
        check_vma=False,
    )
```

time: 1070 us -> 1200 us (1.12)
  Pallas kernels: 0 us -> 1040 us
  waiting for transfers between devices: 441 us -> 0 us
  other arithmetic: 383 us -> 50.1 us
  local copies, waits for them, and re-layouts: 130 us -> 54.3 us
  matrix products: 80 us -> 39.1 us
  between operations: 20.6 us -> 1.05 us
    pallas_call x0 -> x2, Pallas kernels: none -> 1040 us  [the longest x1 982 us: spread(): pl.pallas_call(spread_kernel, out_shape=(jax.ShapeDtypeStruct((2, PW, wid...]
    psum x6 -> x0, waiting for transfers between devices: 441 us -> none  [broadcast(): return lax.psum(block, axis)]
    another operation x44 -> x0, other arithmetic: 353 us -> none  [the longest x29 169 us: body(): factor_local = jnp.linalg.cholesky(diag_block)]
    another operation x115 -> x0, local copies, waits for them, and re-layouts: 59.7 us -> none  [the longest x40 24.6 us: body(): lax.linalg.triangular_solve(lead_block, targets[row_slot], left_side=True...]
    another operation x40 -> x0, matrix products: 35.7 us -> none  [the longest x14 18.5 us: body(): lax.linalg.triangular_solve(corner, column, left_side=False, lower=True,...]
    unnamed x0 -> x4, other arithmetic: none -> 27.8 us
    unnamed x47 -> x26, local copies, waits for them, and re-layouts: 54.1 us -> 31.4 us
  transfers between devices with their start and end apart: 6 -> 0, of which waited for: 6 -> 0; matrix products, arithmetic and copies ran while one was open for 7% -> 0% of each run, Pallas kernels for 0% -> 0%
where the time goes in v1:
time: 1200 us; the launch traced here: 1190 us
  Pallas kernels  1040 us (87%)
  local copies, waits for them, and re-layouts  54.3 us (5%)
  other arithmetic  50.1 us (4%)
  matrix products  39.1 us (3%)
    pallas_call x1, Pallas kernels, spread(): pl.pallas_call(spread_kernel, out_shape=(jax.ShapeDtypeStruct((2, PW, wid...  982 us
    pallas_call x1, Pallas kernels, corner(): pl.pallas_call(corner_kernel, out_shape=jax.ShapeDtypeStruct((NB, NB), jn...  60.5 us
    unnamed x26, local copies, waits for them, and re-layouts  31.4 us
    unnamed x4, other arithmetic  27.8 us

profile of v1, /device:TPU:18, one launch (start us, length us, event | category | flops | bytes accessed | tf_op | source)
XLA Modules:
  0.0 1187.2 jit_solution(8813891086411911365)
XLA Ops:
  2.9 2.1 broadcast_and_fusion
  6.4 2.4 copy.17
  8.8 26.9 %reduce = f32[2,512,4,512]{3,2,1,0:T(4,128)} reduce(f32[2,1,512,4,1,512]{5,4,3,2,1,0:T(1,128)} %param.4, f32[]{:T(128)} %constant.28), dimensions={1,4}, to_apply=%param.4.reduce_sub_computation | reduce | bytes 16777220 | tf_op args[0]
  35.7 7.5 copy.16
  43.2 2.8 select_add_fusion
  46.0 3.4 copy-done.1
  50.9 8.9 copy.20
  59.8 3.7 slice_add_fusion
  63.5 2.0 copy.15
  65.5 2.5 pad_maximum_fusion.1.hsrc
  68.0 982.0 %shard_map.59 = (f32[2,512,2176]{2,1,0:T(8,128)}, f32[2,1024,512]{2,1,0:T(8,128)}, f32[3,512,512]{2,1,0:T(8,128)}) custom-call(f32[512,2176]{1,0:T(8,128)} %pad_maximum_fusion.1.hsrc, f32[1024,512]{1,0:T(8,128)} %slice.79.gsrc), custom_call_target="tpu_custom_call" | custom-call | tf_op jit(solution)/shard_map/pallas_call | solution.py:188
  1050.1 2.8 slice_bitcast_fusion.1
  1053.2 60.5 %shard_map.60 = f32[1024,1024]{1,0:T(8,128)S(1)} custom-call(f32[3,512,512]{2,1,0:T(8,128)S(1)} %copy-done), custom_call_target="tpu_custom_call" | custom-call | tf_op jit(solution)/shard_map/pallas_call | solution.py:286
  1113.7 6.9 fusion
  1120.6 3.4 fusion.4
  1124.1 8.7 fusion.9
  1132.7 20.2 %maximum_subtract_fusion = f32[1024,2176]{1,0:T(8,128)S(1)} fusion(f32[1024,128]{1,0:T(8,128)S(1)} %bitcast.50, f32[1024,2048]{1,0:T(8,128)S(1)} %bitcast.47, f32[1024,1024]{1,0:T(8,128)} %fusion.9, f32[1024,2176]{1,0:T(8,128)} %bitcast.54), kind=kOutput, calls=%fused_computation | convolution fusion | flops 13694664704 | bytes 30932992 | tf_op jit(solution)/shard_map/dot_general | solution.py:313
  1153.0 4.1 slice_select_fusion
  1157.9 2.3 fusion.8
  1162.1 2.9 copy.12
  1165.0 1.9 slice_select_fusion.1
  1166.9 2.8 slice-done
  1169.7 3.8 pad_maximum_fusion
  1173.5 13.5 %reshape.125 = f32[2,1,512,4,1,512]{5,4,3,2,1,0:T(1,128)} reshape(f32[1024,2048]{1,0:T(8,128)} %pad_maximum_fusion) | data formatting | bytes 16777216 | tf_op jit(solution)/shard_map/reshape | solution.py:325
  (35 shorter events, 8.3 us)
Async XLA Ops:
  5.0 1.4 copy-start.2
  35.7 7.5 copy-start.6
  46.0 3.4 copy-start.1
  50.9 8.9 copy-start.3
  1050.1 3.2 copy-start
  1120.6 3.4 copy-start.4
  1120.6 12.1 %slice-start.1 = ((s8[8388608]{0:T(1024)(128)(4,1)}), s8[4194304]{0:T(1024)(128)(4,1)S(1)}, s32[]{:S(2)}) async-start(s8[8388608]{0:T(1024)(128)(4,1)} %bitcast.46), calls=%async_computation.1 | async-start | bytes 8388608
  1124.1 8.7 slice-start.2
  1153.0 4.9 copy-start.5
  1166.9 2.8 slice-start

commit v2 on v0

v2 whole, which is shorter than its diff:
```python
import jax
import jax.numpy as jnp
from jax import lax
from jax.experimental import pallas as pl
from jax.experimental.pallas import tpu as pltpu
from jax.sharding import PartitionSpec as P

MESH = pl.DeviceIdType.MESH
HIGHEST = lax.Precision.HIGHEST
HIGH = lax.Precision.HIGH
PW = 512
NB = 2 * PW
BK = 128
CH = 32
GC = 64

TREES = (
    (1, 11, 9, 0, 0, 7, 1, 0, 0, 4, 1, 0, 0, 4, 9, 0),
    (2, 0, 0, 0, 7, 8, 8, 14, 3, 3, 2, 2, 0, 0, 0, 0),
    (4, 0, 6, 14, 0, 0, 6, 1, 0, 0, 4, 1, 0, 0, 4, 13),
    (8, 0, 0, 0, 0, 0, 0, 0, 12, 8, 8, 12, 13, 11, 2, 2),
)


def tree_table():
    step = ((0, 1), (1, 0), (0, -1), (-1, 0))
    table = []
    for tree in TREES:
        depth = {0: 0}
        stack = [0]
        while stack:
            at = stack.pop()
            for d in range(4):
                if tree[at] >> d & 1:
                    to = (at // 4 + step[d][0]) % 4 * 4 + (at % 4 + step[d][1]) % 4
                    depth[to] = depth[at] + 1
                    stack.append(to)
        table.append([tree[at] | depth[at] << 4 for at in range(16)])
    return table


class Spread:
    SLOTS = 23
    LATE = (0, 1)

    def __init__(self, hsrc, tsrc, gsrc, H, Tg, G, K, hr, hs, tr, ts, kr, ks, gr, gs):
        self.hsrc, self.tsrc, self.gsrc = hsrc, tsrc, gsrc
        self.H, self.Tg, self.G, self.K = H, Tg, G, K
        self.hr, self.hs, self.tr, self.ts = hr, hs, tr, ts
        self.kr, self.ks, self.gr, self.gs = kr, ks, gr, gs
        row, col = lax.axis_index("row"), lax.axis_index("col")
        y, z, x, core = row // 4, row % 4, col // 2, col % 2
        self.row, self.col, self.x, self.core = row, col, x, core
        self.where = [
            (y * 4 + (z + 1) % 4, col),
            (((y + 1) % 4) * 4 + z, col),
            (y * 4 + (z + 3) % 4, col),
            (((y + 3) % 4) * 4 + z, col),
            (row, ((x + 1) % 4) * 2 + core),
            (row, ((x + 3) % 4) * 2 + core),
            (row, x * 2 + 1 - core),
        ]
        self.mask, self.depth = [], []
        for root in range(2):
            place = y * 4 + (z + 4 - root) % 4
            masks, depths = [], []
            for entries in tree_table():
                v = jnp.int32(0)
                for at, entry in enumerate(entries):
                    v = jnp.where(place == at, entry, v)
                masks.append(v & 15)
                depths.append((v >> 4) + self.LATE[root])
            self.mask.append(masks)
            self.depth.append(depths)
        self.hops = [x, (4 - x) % 4]
        self.on = [x != 3, x != 1]

    def remote(self, src, dst, send, recv, to):
        return pltpu.make_async_remote_copy(
            src_ref=src, dst_ref=dst, send_sem=send, recv_sem=recv, device_id=self.where[to], device_id_type=MESH
        )

    def hpiece(self, root, tree, n):
        at = pl.multiple_of((n % 4) * BK + tree * CH, CH)
        return self.H.at[root, pl.ds(at, CH), pl.ds(pl.multiple_of((n // 4) * PW, PW), PW)]

    def hsrc_piece(self, tree, n):
        at = pl.multiple_of((n % 4) * BK + tree * CH, CH)
        return self.hsrc.at[pl.ds(at, CH), pl.ds(pl.multiple_of((n // 4) * PW, PW), PW)]

    def kpiece(self, block, tree, n):
        return self.K.at[block, pl.ds(pl.multiple_of(n * BK + tree * CH, CH), CH), :]

    def gpiece(self, half, g):
        return self.G.at[half, pl.ds(pl.multiple_of(g * GC, GC), GC), :]

    def start(self):
        barrier = pltpu.get_barrier_semaphore()
        for device in self.where:
            pl.semaphore_signal(barrier, inc=1, device_id=device, device_id_type=MESH)
        for root in range(2):

            @pl.when(self.row == root)
            def _():
                def own(n, carry):
                    for tree in range(4):
                        pltpu.make_async_copy(
                            self.hsrc_piece(tree, n), self.hpiece(root, tree, n), self.hr.at[root, tree, n]
                        ).start()
                    return carry

                lax.fori_loop(0, 16, own, 0)
                for tree in range(4):
                    rows = pl.ds(tree * BK, BK)
                    pltpu.make_async_copy(
                        self.tsrc.at[rows, :], self.Tg.at[root, rows, :], self.tr.at[root, tree]
                    ).start()

        for half in range(2):

            @pl.when(self.col == half)
            def _():
                def own(g, carry):
                    rows = pl.ds(pl.multiple_of(g * GC, GC), GC)
                    pltpu.make_async_copy(self.gsrc.at[rows, :], self.gpiece(half, g), self.gr.at[half, g]).start()
                    return carry

                lax.fori_loop(0, 16, own, 0)
        pl.semaphore_wait(barrier, len(self.where))

    def slot(self, s):
        for root in range(2):
            for tree in range(4):
                self.h_slot(root, tree, s - self.depth[root][tree])
        for block in range(3):
            for tree in range(4):
                root, way = block // 2, tree % 2
                n = s - self.depth[root][tree] - self.hops[way]
                here = jnp.logical_and(self.core == min(block, 1), self.x != 0)

                @pl.when(jnp.logical_and(here, jnp.logical_and(n >= 0, n < 4)))
                def _():
                    piece, recv = self.kpiece(block, tree, n), self.kr.at[block, tree, n]
                    self.remote(piece, piece, self.ks.at[block, tree, 0], recv, 6).wait_recv()

                    @pl.when(self.on[way])
                    def _():
                        self.remote(piece, piece, self.ks.at[block, tree, 0], recv, 4 + way).start()

                    self.remote(piece, piece, self.ks.at[block, tree, 1], recv, 6).start()

        for half in range(2):
            for way in range(2):
                t = s - 3 - self.hops[way]
                g = (t // 2) * 2 + way
                valid = jnp.logical_and(jnp.logical_and(t >= 0, t < 16), t % 2 == 0)

                @pl.when(jnp.logical_and(valid, self.core == half))
                def _():
                    piece, recv = self.gpiece(half, g), self.gr.at[half, g]
                    self.remote(piece, piece, self.gs.at[half, way, 0], recv, 6).wait_recv()

                    @pl.when(self.on[way])
                    def _():
                        self.remote(piece, piece, self.gs.at[half, way, 0], recv, 4 + way).start()

                    self.remote(piece, piece, self.gs.at[half, way, 1], recv, 6).start()

    def dirs(self, tree):
        return [d for d in range(4) if any(bits >> d & 1 for bits in TREES[tree])]

    def has(self, root, tree, d):
        return (self.mask[root][tree] >> d) & 1 == 1

    def h_slot(self, root, tree, n):
        @pl.when(jnp.logical_and(n >= 0, n < 16))
        def _():
            piece, recv = self.hpiece(root, tree, n), self.hr.at[root, tree, n]
            self.remote(piece, piece, self.hs.at[root, tree, 0], recv, 0).wait_recv()
            for d in self.dirs(tree):

                @pl.when(self.has(root, tree, d))
                def _():
                    self.remote(piece, piece, self.hs.at[root, tree, d], recv, d).start()

            for core in range(2):
                block = root + core
                if (root, core) == (1, 0):
                    continue

                @pl.when(jnp.logical_and(self.col == core, n < 4))
                def _():
                    m = jnp.minimum(n, 3)
                    to, krecv = self.kpiece(block, tree, m), self.kr.at[block, tree, m]
                    pltpu.make_async_copy(piece, to, krecv).start()
                    self.remote(piece, to, self.ks.at[block, tree, 0], krecv, 4 + tree % 2).start()
                    self.remote(piece, to, self.ks.at[block, tree, 1], krecv, 6).start()

        @pl.when(n == 16)
        def _():
            piece, recv = self.Tg.at[root, pl.ds(tree * BK, BK), :], self.tr.at[root, tree]
            self.remote(piece, piece, self.ts.at[root, tree, 0], recv, 0).wait_recv()
            for d in self.dirs(tree):

                @pl.when(self.has(root, tree, d))
                def _():
                    self.remote(piece, piece, self.ts.at[root, tree, d], recv, d).start()

    def corner_rows(self, block, n):
        @pl.when(jnp.logical_or(self.core != min(block, 1), self.x == 0))
        def _():
            for tree in range(4):
                piece, recv = self.kpiece(block, tree, n), self.kr.at[block, tree, n]
                self.remote(piece, piece, self.ks.at[block, tree, 0], recv, 6).wait_recv()

    def finish(self):
        for half in range(2):

            @pl.when(self.core != half)
            def _():
                def one(g, carry):
                    piece, recv = self.gpiece(half, g), self.gr.at[half, g]
                    self.remote(piece, piece, self.gs.at[half, 0, 0], recv, 6).wait_recv()
                    return carry

                lax.fori_loop(0, 16, one, 0)

            @pl.when(self.core == half)
            def _():
                for way in range(2):
                    whole = self.G.at[half, pl.ds(0, PW), :]
                    wait_sent(self, whole, self.gs.at[half, way, 1])

                    @pl.when(self.on[way])
                    def _():
                        wait_sent(self, whole, self.gs.at[half, way, 0])

        for root in range(2):
            for tree in range(4):
                for d in self.dirs(tree):

                    @pl.when(self.has(root, tree, d))
                    def _():
                        wait_sent(self, self.H.at[root, :, pl.ds(0, PW)], self.hs.at[root, tree, d])
                        wait_sent(self, self.Tg.at[root, pl.ds(tree * BK, BK), :], self.ts.at[root, tree, d])

        for block in range(3):

            @pl.when(self.core == min(block, 1))
            def _():
                for tree in range(4):
                    whole = self.K.at[block, pl.ds(0, BK), :]
                    wait_sent(self, whole, self.ks.at[block, tree, 1])

                    @pl.when(self.on[tree % 2])
                    def _():
                        wait_sent(self, whole, self.ks.at[block, tree, 0])


def wait_sent(spread, whole, sem):
    spread.remote(whole, whole, sem, spread.gr.at[0, 0], 6).wait_send()


def spread_semaphores():
    dma = pltpu.SemaphoreType.DMA
    return [
        dma((2, 4, 16)),
        dma((2, 4, 4)),
        dma((2, 4)),
        dma((2, 4, 4)),
        dma((3, 4, 4)),
        dma((3, 4, 2)),
        dma((2, 16)),
        dma((2, 2, 2)),
    ]


def dot(a, b, dims=((1,), (0,))):
    return lax.dot_general(a, b, (dims, ((), ())), precision=HIGHEST, preferred_element_type=jnp.float32)


def recip(d):
    r = pltpu.reciprocal(d, approx=True)
    return r * (2.0 - d * r)


def factor128(read):
    lane = lax.broadcasted_iota(jnp.int32, (8, BK), 1)
    sub = lax.broadcasted_iota(jnp.int32, (8, BK), 0)
    R = [read(p) for p in range(16)]
    Q = [jnp.where(lane == sub + 8 * p, 1.0, 0.0) for p in range(16)]
    splat = lambda v: jnp.broadcast_to(v, (8, BK))
    W = []
    for p in range(16):
        B = [splat(R[p][:, 8 * p + k : 8 * p + k + 1]) for k in range(8)]
        below = {i: [splat(R[i][:, 8 * p + k : 8 * p + k + 1]) for k in range(8)] for i in range(p + 1, 16)}
        Rp, Qp = R[p], Q[p]
        pivots = None
        for j in range(8):
            d = splat(B[j][j : j + 1, :])
            inv = recip(d)
            pivots = d if pivots is None else jnp.where(sub == j, d, pivots)
            coef = jnp.where(sub > j, B[j] * inv, 0.0)
            ur, qr = splat(Rp[j : j + 1, :]), splat(Qp[j : j + 1, :])
            lead = {k: splat(B[k][j : j + 1, :]) for k in range(j + 1, 8)}
            for i in range(p + 1, 16):
                ci = below[i][j] * inv
                for k in range(j + 1, 8):
                    below[i][k] = below[i][k] - ci * lead[k]
                R[i] = R[i] - ci * ur
                Q[i] = Q[i] - ci * qr
            if j < 7:
                for k in range(j + 1, 8):
                    B[k] = B[k] - coef * lead[k]
                Rp = Rp - coef * ur
                Qp = Qp - coef * qr
        scale = lax.rsqrt(pivots)
        W.append(Qp * scale)
    return W


def split(v):
    hi = v.astype(jnp.bfloat16)
    return hi, (v - hi.astype(jnp.float32)).astype(jnp.bfloat16)


def dot3(a, b, dims=((1,), (0,))):
    one = lambda u, v: lax.dot_general(u, v, (dims, ((), ())), preferred_element_type=jnp.float32)
    return one(a[0], b[0]) + (one(a[0], b[1]) + one(a[1], b[0]))


PRE = 9
PER = 2


def front_kernel(hsrc, tsrc, gsrc, t_out, x_out, h_out, g_out, head_out, H, Tg, G, K, E, D, Gh, Gl, Wh, Wl, out_sem, *sems):
    spread = Spread(hsrc, tsrc, gsrc, H, Tg, G, K, *sems)
    count = NB // BK

    def slots(first, n):
        def one(s, carry):
            spread.slot(s)
            return carry

        lax.fori_loop(first, first + n, one, 0)

    spread.start()
    E[...] = jnp.zeros_like(E)
    slots(0, PRE)
    lane = lax.broadcasted_iota(jnp.int32, (BK, NB), 1)

    def step(k, carry):
        r0 = pl.multiple_of(k * BK, BK)
        rows = pl.ds(r0, BK)
        spread.slot(PRE + PER * k)

        @pl.when(k < 4)
        def _():
            n = jnp.minimum(k, 3)
            spread.corner_rows(0, n)
            spread.corner_rows(1, n)
            at = pl.ds(pl.multiple_of(n * BK, BK), BK)
            E[rows, 0:PW] = E[rows, 0:PW] + jnp.where(lane[:, :PW] >= r0, K[0, at, :], 0.0)
            E[rows, PW:NB] = E[rows, PW:NB] + K[1, at, :]

        @pl.when(k >= 4)
        def _():
            n = jnp.maximum(k - 4, 0)
            spread.corner_rows(2, n)
            at = pl.ds(pl.multiple_of(n * BK, BK), BK)
            E[rows, PW:NB] = E[rows, PW:NB] + jnp.where(lane[:, PW:] >= r0, K[2, at, :], 0.0)

        W = factor128(lambda p: E[pl.ds(r0 + 8 * p, 8), pl.ds(r0, BK)])
        for p in range(16):
            D[pl.ds(8 * p, 8), :] = W[p]
        spread.slot(PRE + PER * k + 1)
        E[rows, :] = dot(D[...], E[rows, :])
        E[rows, pl.ds(r0, BK)] = D[...]
        hi, lo = split(jnp.where(lane < r0 + BK, E[rows, :], 0.0))
        Wh[rows, :] = hi
        Wl[rows, :] = lo

        def under(i, carry):
            i0 = pl.multiple_of(i * BK, BK)
            E[pl.ds(i0, BK), pl.ds(r0, BK)] = jnp.zeros((BK, BK), jnp.float32)
            E[pl.ds(i0, BK), :] = E[pl.ds(i0, BK), :] - dot(E[rows, pl.ds(i0, BK)], E[rows, :], ((0,), (0,)))
            return carry

        lax.fori_loop(k + 1, count, under, 0)
        return carry

    lax.fori_loop(0, count, step, 0)
    spread.finish()
    outs = [pltpu.make_async_copy(H, h_out, out_sem.at[0]), pltpu.make_async_copy(Tg, g_out, out_sem.at[1])]
    for copy in outs:
        copy.start()

    q = PW // 2

    def block(i, carry):
        rows = pl.ds(pl.multiple_of(i * q, q), q)
        gh, gl = [], []
        for half in range(2):
            hi, lo = split(G[half, rows, :])
            Gh[:, half * PW : (half + 1) * PW] = hi
            Gl[:, half * PW : (half + 1) * PW] = lo
        for j in range(4):
            to = pl.ds(j * q, q)
            kk = pl.ds(0, (j + 1) * q)
            E[rows, to] = dot3((Gh[:, kk], Gl[:, kk]), (Wh[to, kk], Wl[to, kk]), ((1,), (1,)))
        hi, lo = split(E[rows, :])
        Gh[...] = hi
        Gl[...] = lo
        for j in range(4):
            kk = pl.ds(j * q, NB - j * q)
            to = pl.ds(j * q, q)
            G[j // 2, rows, pl.ds(j % 2 * q, q)] = dot3((Gh[:, kk], Gl[:, kk]), (Wh[kk, to], Wl[kk, to]))
        return carry

    lax.fori_loop(0, 4, block, 0)
    outs.append(pltpu.make_async_copy(G, t_out, out_sem.at[2]))
    outs[2].start()
    outs.append(pltpu.make_async_copy(E.at[:, pl.ds(pl.multiple_of(spread.core * PW, PW), PW)], x_out, out_sem.at[3]))
    outs[3].start()
    for half in range(2):
        kh = [split(Tg[part]) for part in range(half + 1)]
        total = jnp.zeros((PW, BK), jnp.float32)
        for part in range(half + 1):
            kk = pl.ds(part * PW, PW)
            to = pl.ds(half * PW, PW)
            total = total + dot3((Wh[to, kk], Wl[to, kk]), kh[part])
        K[half, :, 0:BK] = total
    outs.append(pltpu.make_async_copy(K.at[pl.ds(0, 2), :, pl.ds(0, BK)], head_out, out_sem.at[4]))
    outs[4].start()
    for copy in outs:
        copy.wait()


def front(hsrc, tsrc, gsrc):
    f32, bf16 = jnp.float32, jnp.bfloat16
    series = tsrc.shape[1]
    return pl.pallas_call(
        front_kernel,
        out_shape=(
            jax.ShapeDtypeStruct((2, NB, PW), f32),
            jax.ShapeDtypeStruct((NB, PW), f32),
            jax.ShapeDtypeStruct((2, PW, 4 * PW), f32),
            jax.ShapeDtypeStruct((2, PW, series), f32),
            jax.ShapeDtypeStruct((2, PW, series), f32),
        ),
        in_specs=[pl.BlockSpec(memory_space=pl.ANY)] * 3,
        out_specs=[pl.BlockSpec(memory_space=pl.ANY)] * 5,
        scratch_shapes=[
            pltpu.VMEM((2, PW, 4 * PW), f32),
            pltpu.VMEM((2, PW, series), f32),
            pltpu.VMEM((2, NB, PW), f32),
            pltpu.VMEM((3, PW, PW), f32),
            pltpu.VMEM((NB, NB), f32),
            pltpu.VMEM((BK, BK), f32),
            pltpu.VMEM((PW // 2, NB), bf16),
            pltpu.VMEM((PW // 2, NB), bf16),
            pltpu.VMEM((NB, NB), bf16),
            pltpu.VMEM((NB, NB), bf16),
            pltpu.SemaphoreType.DMA((5,)),
        ]
        + spread_semaphores(),
        compiler_params=pltpu.CompilerParams(collective_id=0, has_side_effects=True, vmem_limit_bytes=56 * 2**20),
    )(hsrc, tsrc, gsrc)


def diagonal(block, noise, c, s):
    row, col = lax.axis_index("row"), lax.axis_index("col")
    size = noise.shape[0]
    a, first = block // (PW // size), block % (PW // size) * size
    i = lax.broadcasted_iota(jnp.int32, (size, BK), 0) + first
    j = lax.broadcasted_iota(jnp.int32, (size, BK), 1) + s * BK
    on = a * 16 + row == c * 8 + col
    return jnp.where(jnp.logical_and(i == j, on), noise, 0.0)


def prepare_kernel(cov, noise, hsrc, gsrc):
    block = pl.program_id(0)
    for s in range(16):
        tile = cov[:, s, :]
        if s < 4:
            tile = tile + diagonal(block, noise[...], 0, s)
            gsrc[:, s * BK : (s + 1) * BK] = tile

        @pl.when(block < 4)
        def _():
            hsrc[:, s * BK : (s + 1) * BK] = tile


def prepare(cov, noise):
    return pl.pallas_call(
        prepare_kernel,
        grid=(8,),
        out_shape=(jax.ShapeDtypeStruct((PW, 4 * PW), jnp.float32), jax.ShapeDtypeStruct((NB, PW), jnp.float32)),
        in_specs=[pl.BlockSpec((BK, 16, BK), lambda i: (i, 0, 0)), pl.BlockSpec((BK, 1), lambda i: (i, 0))],
        out_specs=[
            pl.BlockSpec((BK, 4 * PW), lambda i: (jnp.minimum(i, 3), 0)),
            pl.BlockSpec((BK, PW), lambda i: (i, 0)),
        ],
        compiler_params=pltpu.CompilerParams(vmem_limit_bytes=32 * 2**20),
    )(cov, noise)


UR = 256


def update_kernel(cov, noise, T, H, Tg, X, targets, head, out, reduced, Hh, Hl, Sh, Sl):
    step = pl.program_id(0)
    row, col = lax.axis_index("row"), lax.axis_index("col")

    @pl.when(step == 0)
    def _():
        def one(i, carry):
            rows = pl.ds(pl.multiple_of(i * BK, BK), BK)
            Hh[rows, :], Hl[rows, :] = split(H[rows, :])
            Sh[rows, :], Sl[rows, :] = split(Tg[rows, :])
            return carry

        lax.fori_loop(0, NB // BK, one, 0)

    lead = jnp.logical_and(row < 2, step < PW // UR)
    t0, t1 = split(T[0]), split(T[1])

    def minus(hi, lo, c0, n):
        to = pl.ds(c0, n)
        top, low = pl.ds(0, PW), pl.ds(PW, PW)
        return dot3(t0, (hi[top, to], lo[top, to])) + dot3(t1, (hi[low, to], lo[low, to]))

    i = lax.broadcasted_iota(jnp.int32, (UR, BK), 0) + (step // (PW // UR) * 16 + row) * PW + step % (PW // UR) * UR
    for b in range(8):
        d = minus(Hh, Hl, b * 256, 256)
        for e in range(2):
            s = 2 * b + e
            value = cov[:, s, :] + diagonal(step, noise[...], s // 4, s % 4) - d[:, e * BK : (e + 1) * BK]
            value = jnp.where(lead, 0.0, value)
            if s < 4:
                j = lax.broadcasted_iota(jnp.int32, (UR, BK), 1) + col * PW + s * BK
                value = jnp.where(col < 2, jnp.where(i >= j, X[:, s * BK : (s + 1) * BK], 0.0), value)
            out[:, s, :] = value
    reduced[...] = jnp.where(lead, head[...], targets[...] - minus(Sh, Sl, 0, BK))


def update(cov, noise, T, H, Tg, X, targets, head):
    series = targets.shape[1]
    whole = lambda shape: pl.BlockSpec(shape, lambda i: (0,) * len(shape))
    rows = lambda n: pl.BlockSpec((UR, n), lambda i: (i, 0))
    bf16 = jnp.bfloat16
    return pl.pallas_call(
        update_kernel,
        grid=(NB // UR,),
        out_shape=(jax.ShapeDtypeStruct(cov.shape, jnp.float32), jax.ShapeDtypeStruct(targets.shape, jnp.float32)),
        in_specs=[
            pl.BlockSpec((UR, 16, BK), lambda i: (i, 0, 0)),
            rows(1),
            pl.BlockSpec((2, UR, PW), lambda i: (0, i, 0)),
            whole((NB, 4 * PW)),
            whole((NB, series)),
            rows(PW),
            rows(series),
            pl.BlockSpec((UR, series), lambda i: (i % (PW // UR), 0)),
        ],
        out_specs=[pl.BlockSpec((UR, 16, BK), lambda i: (i, 0, 0)), rows(series)],
        scratch_shapes=[
            pltpu.VMEM((NB, 4 * PW), bf16),
            pltpu.VMEM((NB, 4 * PW), bf16),
            pltpu.VMEM((NB, series), bf16),
            pltpu.VMEM((NB, series), bf16),
        ],
        compiler_params=pltpu.CompilerParams(vmem_limit_bytes=56 * 2**20),
    )(cov, noise, T, H, Tg, X, targets, head)


def body(covariance, noise_var, observed, cloud_free):
    row = lax.axis_index("row")
    series = observed.shape[3]
    cov = covariance.reshape(NB, 16, BK)
    noise = noise_var.reshape(NB, 1)
    targets = (observed * cloud_free.astype(jnp.float32)).reshape(NB, series)
    hsrc, gsrc = prepare(cov, noise)
    T, X, H, Tg, head = front(hsrc, targets[:PW], gsrc)
    head = jnp.where(row == 0, head[0], head[1])
    factor, reduced = update(cov, noise, T, H.reshape(NB, 4 * PW), Tg.reshape(NB, series), X, targets, head)
    return factor.reshape(covariance.shape), reduced.reshape(observed.shape)


def solution(mesh):
    placed = (
        P(None, "row", None, None, "col", None),
        P(None, "row", None),
        P(None, "row", None, "col"),
        P(None, "row", None, "col"),
    )
    return jax.shard_map(
        body,
        mesh=mesh,
        in_specs=placed,
        out_specs=(P(None, "row", None, None, "col", None), P(None, "row", None, "col")),
        check_vma=False,
    )
```

time: 1070 us -> 191 us (0.18); the launches traced: 1060 us -> 191 us
  waiting for transfers between devices: 441 us -> 0 us
  other arithmetic: 383 us -> 3.23 us
  Pallas kernels: 0 us -> 178 us
  local copies, waits for them, and re-layouts: 130 us -> 8.39 us
  matrix products: 80 us -> 0 us
  between operations: 20.6 us -> 0.71 us
    psum x6 -> x0, waiting for transfers between devices: 441 us -> none  [broadcast(): return lax.psum(block, axis)]
    another operation x44 -> x0, other arithmetic: 353 us -> none  [the longest x29 169 us: body(): factor_local = jnp.linalg.cholesky(diag_block)]
    pallas_call x0 -> x3, Pallas kernels: none -> 178 us  [the longest x1 139 us: front(): pl.pallas_call(front_kernel, out_shape=(jax.ShapeDtypeStruct((2, NB, PW),...]
    another operation x115 -> x0, local copies, waits for them, and re-layouts: 59.7 us -> none  [the longest x40 24.6 us: body(): lax.linalg.triangular_solve(lead_block, targets[row_slot], left_side=True...]
    unnamed x47 -> x10, local copies, waits for them, and re-layouts: 54.1 us -> 6.71 us
    dot_general x4 -> x0, matrix products: 44.3 us -> none  [the longest x2 36.6 us: body(): jnp.einsum('aik,cjk->aicj', left_masked, right_masked, precision=HIGHEST)]
    another operation x40 -> x0, matrix products: 35.7 us -> none  [the longest x14 18.5 us: body(): lax.linalg.triangular_solve(corner, column, left_side=False, lower=True,...]
    select_n x11 -> x1, other arithmetic: 15.1 us -> 1.79 us  [body(): head = jnp.where(row == 0, head[0], head[1])]
  transfers between devices with their start and end apart: 6 -> 0, of which waited for: 6 -> 0; matrix products, arithmetic and copies ran while one was open for 7% -> 0% of each run, Pallas kernels for 0% -> 0%
where the time goes in v2:
time: 191 us
  Pallas kernels  178 us (93%)
  local copies, waits for them, and re-layouts  8.39 us (4%)
  other arithmetic  3.23 us (2%)
    pallas_call x1, Pallas kernels, front(): pl.pallas_call(front_kernel, out_shape=(jax.ShapeDtypeStruct((2, NB, PW),...  139 us
    pallas_call x1, Pallas kernels, update(): pl.pallas_call(update_kernel, grid=(NB // UR,), out_shape=(jax.ShapeDtype...  31.8 us
    pallas_call x1, Pallas kernels, prepare(): pl.pallas_call(prepare_kernel, grid=(8,), out_shape=(jax.ShapeDtypeStruct...  7.68 us
    unnamed x10, local copies, waits for them, and re-layouts  6.71 us

profile of v2, /device:TPU:18, one launch (start us, length us, event | category | flops | bytes accessed | tf_op | source)
XLA Modules:
  0.0 190.6 jit_solution(9301957574630945730)
XLA Ops:
  0.6 0.9 copy.9.noise
  1.5 0.0 copy-start.1
  1.6 1.4 convert_multiply_fusion
  3.0 0.0 copy-start.4
  3.0 0.8 slice_bitcast_fusion.tsrc
  3.8 0.0 copy-start
  3.8 3.4 %copy-done = f32[2,1,512,4,1,512]{5,4,3,2,1,0:T(1,128)S(1)} copy-done((f32[2,1,512,4,1,512]{5,4,3,2,1,0:T(1,128)S(1)}, f32[2,1,512,4,1,512]{5,4,3,2,1,0:T(1,128)}, u32[]{:S(2)}) %copy-start) | copy-done | bytes 8388632
  7.2 7.7 %shard_map.59 = (f32[512,2048]{1,0:T(8,128)S(1)}, f32[1024,512]{1,0:T(8,128)S(1)}) custom-call(f32[1024,16,128]{2,1,0:T(8,128)S(1)} %bitcast.14, f32[1024,1]{1,0:T(8,128)S(1)} %copy.9.noise), custom_call_target="tpu_custom_call" | custom-call | tf_op jit(solution)/shard_map/pallas_call | solution.py:495
  14.9 0.0 copy-done.1
  14.9 0.0 copy-done.4
  14.9 0.0 copy-start.2
  14.9 2.0 %copy-done.2 = f32[512,2048]{1,0:T(8,128)} copy-done((f32[512,2048]{1,0:T(8,128)}, f32[512,2048]{1,0:T(8,128)S(1)}, u32[]{:S(2)}) %copy-start.2) | copy-done | bytes 4194328
  16.9 0.0 copy-start.3
  16.9 1.3 copy-done.3
  18.2 138.8 %shard_map.60 = (f32[2,1024,512]{2,1,0:T(8,128)}, f32[1024,512]{1,0:T(8,128)}, f32[2,512,2048]{2,1,0:T(8,128)}, f32[2,512,128]{2,1,0:T(8,128)}, f32[2,512,128]{2,1,0:T(8,128)}) custom-call(f32[512,2048]{1,0:T(8,128)} %copy-done.2, f32[512,128]{1,0:T(8,128)} %slice_bitcast_fusion.tsrc, f32[1024,512]{1,0:T(8,128)} %copy-done.3), custom_call_target="tpu_custom_call" | custom-call | tf_op jit(solution)/shard_map/pallas_call | solution.py:442
  157.0 1.8 select_bitcast_fusion.head
  158.8 31.8 %shard_map.61 = (f32[1024,16,128]{2,1,0:T(8,128)}, f32[1024,128]{1,0:T(8,128)}) custom-call(f32[1024,16,128]{2,1,0:T(8,128)} %bitcast.13, f32[1024,1]{1,0:T(8,128)} %copy-done.1, f32[2,1024,512]{2,1,0:T(8,128)} %get-tuple-element.13.T, f32[1024,2048]{1,0:T(8,128)} %bitcast.15, f32[1024,128]{1,0:T(8,128)} %bitcast.17, f32[1024,512]{1,0:T(8,128)} %get-tuple-element.16.X, ...), custom_call_target="tpu_custom_call" | custom-call | tf_op jit(solution)/shard_map/pallas_call | solution.py:552
Async XLA Ops:
  1.5 13.3 %copy-start.1 = (f32[1024,1]{1,0:T(8,128)}, f32[1024,1]{1,0:T(8,128)S(1)}, u32[]{:S(2)}) copy-start(f32[1024,1]{1,0:T(8,128)S(1)} %copy.9.noise) | copy-start | bytes 12292
  3.0 11.9 %copy-start.4 = (f32[2,1,512,128]{3,2,1,0:T(8,128)}, f32[2,1,512,128]{3,2,1,0:T(8,128)S(1)}, u32[]{:S(2)}) copy-start(f32[2,1,512,128]{3,2,1,0:T(8,128)S(1)} %convert_multiply_fusion) | copy-start | bytes 1572868
  3.8 3.4 %copy-start = (f32[2,1,512,4,1,512]{5,4,3,2,1,0:T(1,128)S(1)}, f32[2,1,512,4,1,512]{5,4,3,2,1,0:T(1,128)}, u32[]{:S(2)}) copy-start(f32[2,1,512,4,1,512]{5,4,3,2,1,0:T(1,128)} %param.4) | copy-start | bytes 25165828
  14.9 2.0 %copy-start.2 = (f32[512,2048]{1,0:T(8,128)}, f32[512,2048]{1,0:T(8,128)S(1)}, u32[]{:S(2)}) copy-start(f32[512,2048]{1,0:T(8,128)S(1)} %get-tuple-element.11.hsrc) | copy-start | bytes 12582916
  16.9 1.3 copy-start.3

commit v3 on v2

--- a/solution.py
+++ b/solution.py
@@ -40,11 +40,11 @@
 
 
 class Spread:
-    SLOTS = 23
-    LATE = (0, 1)
-
-    def __init__(self, hsrc, tsrc, gsrc, H, Tg, G, K, hr, hs, tr, ts, kr, ks, gr, gs):
-        self.hsrc, self.tsrc, self.gsrc = hsrc, tsrc, gsrc
+    LATE = (0, 4)
+    GLATE = 9
+
+    def __init__(self, cov, noise, tsrc, H, Tg, G, K, own, hr, hs, tr, ts, kr, ks, gr, gs):
+        self.cov, self.noise, self.tsrc, self.own = cov, noise, tsrc, own
         self.H, self.Tg, self.G, self.K = H, Tg, G, K
         self.hr, self.hs, self.tr, self.ts = hr, hs, tr, ts
         self.kr, self.ks, self.gr, self.gs = kr, ks, gr, gs
@@ -69,7 +69,7 @@
                 for at, entry in enumerate(entries):
                     v = jnp.where(place == at, entry, v)
                 masks.append(v & 15)
-                depths.append((v >> 4) + self.LATE[root])
+                depths.append(v >> 4)
             self.mask.append(masks)
             self.depth.append(depths)
         self.hops = [x, (4 - x) % 4]
@@ -82,47 +82,59 @@
 
     def hpiece(self, root, tree, n):
         at = pl.multiple_of((n % 4) * BK + tree * CH, CH)
-        return self.H.at[root, pl.ds(at, CH), pl.ds(pl.multiple_of((n // 4) * PW, PW), PW)]
-
-    def hsrc_piece(self, tree, n):
-        at = pl.multiple_of((n % 4) * BK + tree * CH, CH)
-        return self.hsrc.at[pl.ds(at, CH), pl.ds(pl.multiple_of((n // 4) * PW, PW), PW)]
+        return self.H.at[root, pl.ds(at, CH), n // 4]
 
     def kpiece(self, block, tree, n):
-        return self.K.at[block, pl.ds(pl.multiple_of(n * BK + tree * CH, CH), CH), :]
+        return self.K.at[block, pl.ds(pl.multiple_of(n * BK + tree * CH, CH), CH)]
 
     def gpiece(self, half, g):
-        return self.G.at[half, pl.ds(pl.multiple_of(g * GC, GC), GC), :]
+        return self.G.at[half, g // 8, pl.ds(pl.multiple_of(g % 8 * GC, GC), GC)]
 
     def start(self):
         barrier = pltpu.get_barrier_semaphore()
         for device in self.where:
             pl.semaphore_signal(barrier, inc=1, device_id=device, device_id_type=MESH)
         for root in range(2):
+            corner = pltpu.make_async_copy(self.cov.at[0, :, 0], self.H.at[root, :, 0], self.own)
 
             @pl.when(self.row == root)
             def _():
+                corner.start()
+
                 def own(n, carry):
                     for tree in range(4):
+                        at = pl.multiple_of((n % 4) * BK + tree * CH, CH)
                         pltpu.make_async_copy(
-                            self.hsrc_piece(tree, n), self.hpiece(root, tree, n), self.hr.at[root, tree, n]
+                            self.cov.at[0, pl.ds(at, CH), n // 4],
+                            self.hpiece(root, tree, n),
+                            self.hr.at[root, tree, n],
                         ).start()
                     return carry
 
-                lax.fori_loop(0, 16, own, 0)
+                lax.fori_loop(4, 16, own, 0)
                 for tree in range(4):
                     rows = pl.ds(tree * BK, BK)
                     pltpu.make_async_copy(
                         self.tsrc.at[rows, :], self.Tg.at[root, rows, :], self.tr.at[root, tree]
                     ).start()
+                corner.wait()
+
+            @pl.when(jnp.logical_and(self.row == root, self.col == root))
+            def _():
+                for s in range(4):
+                    rows = pl.ds(s * BK, BK)
+                    self.H[root, rows, 0, s, :] = self.H[root, rows, 0, s, :] + on_diagonal(self.noise[s : s + 1, :])
 
         for half in range(2):
 
             @pl.when(self.col == half)
             def _():
                 def own(g, carry):
-                    rows = pl.ds(pl.multiple_of(g * GC, GC), GC)
-                    pltpu.make_async_copy(self.gsrc.at[rows, :], self.gpiece(half, g), self.gr.at[half, g]).start()
+                    pltpu.make_async_copy(
+                        self.cov.at[g // 8, pl.ds(pl.multiple_of(g % 8 * GC, GC), GC), 0],
+                        self.gpiece(half, g),
+                        self.gr.at[half, g],
+                    ).start()
                     return carry
 
                 lax.fori_loop(0, 16, own, 0)
@@ -131,11 +143,12 @@
     def slot(self, s):
         for root in range(2):
             for tree in range(4):
-                self.h_slot(root, tree, s - self.depth[root][tree])
+                depth, late = self.depth[root][tree], s - self.LATE[root]
+                self.h_slot(root, tree, jnp.where(late - depth < 4, late - depth, jnp.where(late - 2 * depth < 4, -1, late - 2 * depth)))
         for block in range(3):
             for tree in range(4):
                 root, way = block // 2, tree % 2
-                n = s - self.depth[root][tree] - self.hops[way]
+                n = s - self.LATE[root] - self.depth[root][tree] - self.hops[way]
                 here = jnp.logical_and(self.core == min(block, 1), self.x != 0)
 
                 @pl.when(jnp.logical_and(here, jnp.logical_and(n >= 0, n < 4)))
@@ -151,7 +164,7 @@
 
         for half in range(2):
             for way in range(2):
-                t = s - 3 - self.hops[way]
+                t = s - self.GLATE - 2 * self.hops[way]
                 g = (t // 2) * 2 + way
                 valid = jnp.logical_and(jnp.logical_and(t >= 0, t < 16), t % 2 == 0)
 
@@ -176,7 +189,11 @@
         @pl.when(jnp.logical_and(n >= 0, n < 16))
         def _():
             piece, recv = self.hpiece(root, tree, n), self.hr.at[root, tree, n]
-            self.remote(piece, piece, self.hs.at[root, tree, 0], recv, 0).wait_recv()
+
+            @pl.when(jnp.logical_or(self.row != root, n >= 4))
+            def _():
+                self.remote(piece, piece, self.hs.at[root, tree, 0], recv, 0).wait_recv()
+
             for d in self.dirs(tree):
 
                 @pl.when(self.has(root, tree, d))
@@ -228,7 +245,7 @@
             @pl.when(self.core == half)
             def _():
                 for way in range(2):
-                    whole = self.G.at[half, pl.ds(0, PW), :]
+                    whole = self.G.at[half, 0]
                     wait_sent(self, whole, self.gs.at[half, way, 1])
 
                     @pl.when(self.on[way])
@@ -241,7 +258,7 @@
 
                     @pl.when(self.has(root, tree, d))
                     def _():
-                        wait_sent(self, self.H.at[root, :, pl.ds(0, PW)], self.hs.at[root, tree, d])
+                        wait_sent(self, self.H.at[root, :, 0], self.hs.at[root, tree, d])
                         wait_sent(self, self.Tg.at[root, pl.ds(tree * BK, BK), :], self.ts.at[root, tree, d])
 
         for block in range(3):
@@ -249,7 +266,7 @@
             @pl.when(self.core == min(block, 1))
             def _():
                 for tree in range(4):
-                    whole = self.K.at[block, pl.ds(0, BK), :]
+                    whole = self.K.at[block, pl.ds(0, BK)]
                     wait_sent(self, whole, self.ks.at[block, tree, 1])
 
                     @pl.when(self.on[tree % 2])
@@ -257,6 +274,12 @@
                         wait_sent(self, whole, self.ks.at[block, tree, 0])
 
 
+def on_diagonal(line):
+    i = lax.broadcasted_iota(jnp.int32, (BK, BK), 0)
+    j = lax.broadcasted_iota(jnp.int32, (BK, BK), 1)
+    return jnp.where(i == j, line, 0.0)
+
+
 def wait_sent(spread, whole, sem):
     spread.remote(whole, whole, sem, spread.gr.at[0, 0], 6).wait_send()
 
@@ -264,6 +287,7 @@
 def spread_semaphores():
     dma = pltpu.SemaphoreType.DMA
     return [
+        dma,
         dma((2, 4, 16)),
         dma((2, 4, 4)),
         dma((2, 4)),
@@ -284,7 +308,7 @@
     return r * (2.0 - d * r)
 
 
-def factor128(read):
+def factor128(read, halfway):
     lane = lax.broadcasted_iota(jnp.int32, (8, BK), 1)
     sub = lax.broadcasted_iota(jnp.int32, (8, BK), 0)
     R = [read(p) for p in range(16)]
@@ -292,6 +316,8 @@
     splat = lambda v: jnp.broadcast_to(v, (8, BK))
     W = []
     for p in range(16):
+        if p == 8:
+            halfway()
         B = [splat(R[p][:, 8 * p + k : 8 * p + k + 1]) for k in range(8)]
         below = {i: [splat(R[i][:, 8 * p + k : 8 * p + k + 1]) for k in range(8)] for i in range(p + 1, 16)}
         Rp, Qp = R[p], Q[p]
@@ -330,11 +356,11 @@
 
 
 PRE = 9
-PER = 2
-
-
-def front_kernel(hsrc, tsrc, gsrc, t_out, x_out, h_out, g_out, head_out, H, Tg, G, K, E, D, Gh, Gl, Wh, Wl, out_sem, *sems):
-    spread = Spread(hsrc, tsrc, gsrc, H, Tg, G, K, *sems)
+PER = 3
+
+
+def front_kernel(cov, noise, tsrc, t_out, x_out, h_out, g_out, head_out, H, Tg, G, K, E, T, D, Gh, Gl, Wh, Wl, Hd, out_sem, *sems):
+    spread = Spread(cov, noise, tsrc, H, Tg, G, K, *sems)
     count = NB // BK
 
     def slots(first, n):
@@ -344,6 +370,7 @@
 
         lax.fori_loop(first, first + n, one, 0)
 
+    K2, G2 = K.reshape(3 * PW * 4, BK), G.reshape(2 * NB * 4, BK)
     spread.start()
     E[...] = jnp.zeros_like(E)
     slots(0, PRE)
@@ -359,21 +386,25 @@
             n = jnp.minimum(k, 3)
             spread.corner_rows(0, n)
             spread.corner_rows(1, n)
-            at = pl.ds(pl.multiple_of(n * BK, BK), BK)
-            E[rows, 0:PW] = E[rows, 0:PW] + jnp.where(lane[:, :PW] >= r0, K[0, at, :], 0.0)
-            E[rows, PW:NB] = E[rows, PW:NB] + K[1, at, :]
+            for s in range(4):
+                to = slice(s * BK, (s + 1) * BK)
+                E[rows, to] = E[rows, to] + jnp.where(lane[:, to] >= r0, K2[pl.ds(n * (BK * 4) + s, BK, stride=4), :], 0.0)
+            for s in range(4):
+                to = slice(PW + s * BK, PW + (s + 1) * BK)
+                E[rows, to] = E[rows, to] + K2[pl.ds((PW + n * BK) * 4 + s, BK, stride=4), :]
 
         @pl.when(k >= 4)
         def _():
             n = jnp.maximum(k - 4, 0)
             spread.corner_rows(2, n)
-            at = pl.ds(pl.multiple_of(n * BK, BK), BK)
-            E[rows, PW:NB] = E[rows, PW:NB] + jnp.where(lane[:, PW:] >= r0, K[2, at, :], 0.0)
-
-        W = factor128(lambda p: E[pl.ds(r0 + 8 * p, 8), pl.ds(r0, BK)])
+            for s in range(4):
+                to = slice(PW + s * BK, PW + (s + 1) * BK)
+                E[rows, to] = E[rows, to] + jnp.where(lane[:, to] >= r0, K2[pl.ds((2 * PW + n * BK) * 4 + s, BK, stride=4), :], 0.0)
+
+        W = factor128(lambda p: E[pl.ds(r0 + 8 * p, 8), pl.ds(r0, BK)], lambda: spread.slot(PRE + PER * k + 1))
         for p in range(16):
             D[pl.ds(8 * p, 8), :] = W[p]
-        spread.slot(PRE + PER * k + 1)
+        spread.slot(PRE + PER * k + 2)
         E[rows, :] = dot(D[...], E[rows, :])
         E[rows, pl.ds(r0, BK)] = D[...]
         hi, lo = split(jnp.where(lane < r0 + BK, E[rows, :], 0.0))
@@ -400,10 +431,17 @@
     def block(i, carry):
         rows = pl.ds(pl.multiple_of(i * q, q), q)
         gh, gl = [], []
+        mine = jnp.logical_and(spread.row == spread.col, i < 2)
         for half in range(2):
-            hi, lo = split(G[half, rows, :])
-            Gh[:, half * PW : (half + 1) * PW] = hi
-            Gl[:, half * PW : (half + 1) * PW] = lo
+            for s in range(4):
+                for e in range(2):
+                    value = G2[pl.ds((half * NB + i * q + e * BK) * 4 + s, BK, stride=4), :]
+                    here = jnp.logical_and(jnp.logical_and(mine, spread.row == half), i % 2 * 2 + e == s)
+                    value = value + jnp.where(here, on_diagonal(noise[s : s + 1, :]), 0.0)
+                    hi, lo = split(value)
+                    to = slice(half * PW + s * BK, half * PW + (s + 1) * BK)
+                    Gh[e * BK : (e + 1) * BK, to] = hi
+                    Gl[e * BK : (e + 1) * BK, to] = lo
         for j in range(4):
             to = pl.ds(j * q, q)
             kk = pl.ds(0, (j + 1) * q)
@@ -414,11 +452,11 @@
         for j in range(4):
             kk = pl.ds(j * q, NB - j * q)
             to = pl.ds(j * q, q)
-            G[j // 2, rows, pl.ds(j % 2 * q, q)] = dot3((Gh[:, kk], Gl[:, kk]), (Wh[kk, to], Wl[kk, to]))
+            T[rows, to] = dot3((Gh[:, kk], Gl[:, kk]), (Wh[kk, to], Wl[kk, to]))
         return carry
 
     lax.fori_loop(0, 4, block, 0)
-    outs.append(pltpu.make_async_copy(G, t_out, out_sem.at[2]))
+    outs.append(pltpu.make_async_copy(T, t_out, out_sem.at[2]))
     outs[2].start()
     outs.append(pltpu.make_async_copy(E.at[:, pl.ds(pl.multiple_of(spread.core * PW, PW), PW)], x_out, out_sem.at[3]))
     outs[3].start()
@@ -429,80 +467,49 @@
             kk = pl.ds(part * PW, PW)
             to = pl.ds(half * PW, PW)
             total = total + dot3((Wh[to, kk], Wl[to, kk]), kh[part])
-        K[half, :, 0:BK] = total
-    outs.append(pltpu.make_async_copy(K.at[pl.ds(0, 2), :, pl.ds(0, BK)], head_out, out_sem.at[4]))
+        Hd[half] = total
+    outs.append(pltpu.make_async_copy(Hd, head_out, out_sem.at[4]))
     outs[4].start()
     for copy in outs:
         copy.wait()
 
 
-def front(hsrc, tsrc, gsrc):
+def front(cov, noise, tsrc):
     f32, bf16 = jnp.float32, jnp.bfloat16
     series = tsrc.shape[1]
     return pl.pallas_call(
         front_kernel,
         out_shape=(
-            jax.ShapeDtypeStruct((2, NB, PW), f32),
+            jax.ShapeDtypeStruct((NB, NB), f32),
             jax.ShapeDtypeStruct((NB, PW), f32),
-            jax.ShapeDtypeStruct((2, PW, 4 * PW), f32),
+            jax.ShapeDtypeStruct((2, PW, 4, 4, BK), f32),
             jax.ShapeDtypeStruct((2, PW, series), f32),
             jax.ShapeDtypeStruct((2, PW, series), f32),
         ),
-        in_specs=[pl.BlockSpec(memory_space=pl.ANY)] * 3,
+        in_specs=[
+            pl.BlockSpec(memory_space=pl.ANY),
+            pl.BlockSpec(memory_space=pltpu.VMEM),
+            pl.BlockSpec(memory_space=pl.ANY),
+        ],
         out_specs=[pl.BlockSpec(memory_space=pl.ANY)] * 5,
         scratch_shapes=[
-            pltpu.VMEM((2, PW, 4 * PW), f32),
+            pltpu.VMEM((2, PW, 4, 4, BK), f32),
             pltpu.VMEM((2, PW, series), f32),
-            pltpu.VMEM((2, NB, PW), f32),
-            pltpu.VMEM((3, PW, PW), f32),
+            pltpu.VMEM((2, 2, PW, 4, BK), f32),
+            pltpu.VMEM((3, PW, 4, BK), f32),
+            pltpu.VMEM((NB, NB), f32),
             pltpu.VMEM((NB, NB), f32),
             pltpu.VMEM((BK, BK), f32),
             pltpu.VMEM((PW // 2, NB), bf16),
             pltpu.VMEM((PW // 2, NB), bf16),
             pltpu.VMEM((NB, NB), bf16),
             pltpu.VMEM((NB, NB), bf16),
+            pltpu.VMEM((2, PW, series), f32),
             pltpu.SemaphoreType.DMA((5,)),
         ]
         + spread_semaphores(),
         compiler_params=pltpu.CompilerParams(collective_id=0, has_side_effects=True, vmem_limit_bytes=56 * 2**20),
-    )(hsrc, tsrc, gsrc)
-
-
-def diagonal(block, noise, c, s):
-    row, col = lax.axis_index("row"), lax.axis_index("col")
-    size = noise.shape[0]
-    a, first = block // (PW // size), block % (PW // size) * size
-    i = lax.broadcasted_iota(jnp.int32, (size, BK), 0) + first
-    j = lax.broadcasted_iota(jnp.int32, (size, BK), 1) + s * BK
-    on = a * 16 + row == c * 8 + col
-    return jnp.where(jnp.logical_and(i == j, on), noise, 0.0)
-
-
-def prepare_kernel(cov, noise, hsrc, gsrc):
-    block = pl.program_id(0)
-    for s in range(16):
-        tile = cov[:, s, :]
-        if s < 4:
-            tile = tile + diagonal(block, noise[...], 0, s)
-            gsrc[:, s * BK : (s + 1) * BK] = tile
-
-        @pl.when(block < 4)
-        def _():
-            hsrc[:, s * BK : (s + 1) * BK] = tile
-
-
-def prepare(cov, noise):
-    return pl.pallas_call(
-        prepare_kernel,
-        grid=(8,),
-        out_shape=(jax.ShapeDtypeStruct((PW, 4 * PW), jnp.float32), jax.ShapeDtypeStruct((NB, PW), jnp.float32)),
-        in_specs=[pl.BlockSpec((BK, 16, BK), lambda i: (i, 0, 0)), pl.BlockSpec((BK, 1), lambda i: (i, 0))],
-        out_specs=[
-            pl.BlockSpec((BK, 4 * PW), lambda i: (jnp.minimum(i, 3), 0)),
-            pl.BlockSpec((BK, PW), lambda i: (i, 0)),
-        ],
-        compiler_params=pltpu.CompilerParams(vmem_limit_bytes=32 * 2**20),
-    )(cov, noise)
+    )(cov, noise, tsrc)
 
 
 UR = 256
@@ -516,14 +523,16 @@
     def _():
         def one(i, carry):
             rows = pl.ds(pl.multiple_of(i * BK, BK), BK)
-            Hh[rows, :], Hl[rows, :] = split(H[rows, :])
+            for s in range(16):
+                to = slice(s * BK, (s + 1) * BK)
+                Hh[rows, to], Hl[rows, to] = split(H[pl.ds(i * (BK * 16) + s, BK, stride=16), :])
             Sh[rows, :], Sl[rows, :] = split(Tg[rows, :])
             return carry
 
         lax.fori_loop(0, NB // BK, one, 0)
 
     lead = jnp.logical_and(row < 2, step < PW // UR)
-    t0, t1 = split(T[0]), split(T[1])
+    t0, t1 = split(T[:, 0:PW]), split(T[:, PW:NB])
 
     def minus(hi, lo, c0, n):
         to = pl.ds(c0, n)
@@ -531,39 +540,42 @@
         return dot3(t0, (hi[top, to], lo[top, to])) + dot3(t1, (hi[low, to], lo[low, to]))
 
     i = lax.broadcasted_iota(jnp.int32, (UR, BK), 0) + (step // (PW // UR) * 16 + row) * PW + step % (PW // UR) * UR
+    shifted = lax.broadcasted_iota(jnp.int32, (UR, BK), 0) - lax.broadcasted_iota(jnp.int32, (UR, BK), 1)
     for b in range(8):
         d = minus(Hh, Hl, b * 256, 256)
         for e in range(2):
             s = 2 * b + e
-            value = cov[:, s, :] + diagonal(step, noise[...], s // 4, s % 4) - d[:, e * BK : (e + 1) * BK]
+            on = jnp.logical_and(step // 2 * 16 + row == s // 4 * 8 + col, step % 2 == s % 4 // 2)
+            line = jnp.where(on, noise[pl.ds(step // 2 * 4 + s % 4, 1), :], 0.0)
+            value = cov[pl.ds(s, UR, stride=16), :] + jnp.where(shifted == s % 2 * BK, line, 0.0) - d[:, e * BK : (e + 1) * BK]
             value = jnp.where(lead, 0.0, value)
             if s < 4:
                 j = lax.broadcasted_iota(jnp.int32, (UR, BK), 1) + col * PW + s * BK
                 value = jnp.where(col < 2, jnp.where(i >= j, X[:, s * BK : (s + 1) * BK], 0.0), value)
-            out[:, s, :] = value
-    reduced[...] = jnp.where(lead, head[...], targets[...] - minus(Sh, Sl, 0, BK))
+            out[pl.ds(s, UR, stride=16), :] = value
+    reduced[...] = jnp.where(lead, jnp.where(row == 0, head[0], head[1]), targets[...] - minus(Sh, Sl, 0, BK))
 
 
 def update(cov, noise, T, H, Tg, X, targets, head):
     series = targets.shape[1]
     whole = lambda shape: pl.BlockSpec(shape, lambda i: (0,) * len(shape))
-    rows = lambda n: pl.BlockSpec((UR, n), lambda i: (i, 0))
+    rows = lambda n, m=1: pl.BlockSpec((UR * m, n), lambda i: (i, 0))
     bf16 = jnp.bfloat16
     return pl.pallas_call(
         update_kernel,
         grid=(NB // UR,),
         out_shape=(jax.ShapeDtypeStruct(cov.shape, jnp.float32), jax.ShapeDtypeStruct(targets.shape, jnp.float32)),
         in_specs=[
-            pl.BlockSpec((UR, 16, BK), lambda i: (i, 0, 0)),
-            rows(1),
-            pl.BlockSpec((2, UR, PW), lambda i: (0, i, 0)),
-            whole((NB, 4 * PW)),
+            rows(BK, 16),
+            whole((8, BK)),
+            rows(NB),
+            whole((NB * 16, BK)),
             whole((NB, series)),
             rows(PW),
             rows(series),
-            pl.BlockSpec((UR, series), lambda i: (i % (PW // UR), 0)),
+            pl.BlockSpec((2, UR, series), lambda i: (0, i % (PW // UR), 0)),
         ],
-        out_specs=[pl.BlockSpec((UR, 16, BK), lambda i: (i, 0, 0)), rows(series)],
+        out_specs=[rows(BK, 16), rows(series)],
         scratch_shapes=[
             pltpu.VMEM((NB, 4 * PW), bf16),
             pltpu.VMEM((NB, 4 * PW), bf16),
@@ -575,15 +587,13 @@
 
 
 def body(covariance, noise_var, observed, cloud_free):
-    row = lax.axis_index("row")
     series = observed.shape[3]
-    cov = covariance.reshape(NB, 16, BK)
-    noise = noise_var.reshape(NB, 1)
+    noise = noise_var.reshape(8, BK)
     targets = (observed * cloud_free.astype(jnp.float32)).reshape(NB, series)
-    hsrc, gsrc = prepare(cov, noise)
-    T, X, H, Tg, head = front(hsrc, targets[:PW], gsrc)
-    head = jnp.where(row == 0, head[0], head[1])
-    factor, reduced = update(cov, noise, T, H.reshape(NB, 4 * PW), Tg.reshape(NB, series), X, targets, head)
+    T, X, H, Tg, head = front(covariance.reshape(2, PW, 4, 4, BK), noise, targets[:PW])
+    factor, reduced = update(
+        covariance.reshape(NB * 16, BK), noise, T, H.reshape(NB * 16, BK), Tg.reshape(NB, series), X, targets, head
+    )
     return factor.reshape(covariance.shape), reduced.reshape(observed.shape)
 
 

time: 191 us -> 172 us (0.901)
  Pallas kernels: 178 us -> 169 us
  local copies, waits for them, and re-layouts: 8.39 us -> 0.78 us
  other arithmetic: 3.23 us -> 1.25 us
    unnamed x10 -> x2, local copies, waits for them, and re-layouts: 6.71 us -> 0.01 us
    pallas_call x2 -> x1, Pallas kernels: 146 us -> 141 us  [front(): pl.pallas_call(front_kernel, out_shape=(jax.ShapeDtypeStruct((NB, NB), f3...]
    pallas_call x1, Pallas kernels: 31.8 us -> 28.4 us  [update(): pl.pallas_call(update_kernel, grid=(NB // UR,), out_shape=(jax.ShapeDtype...]
where the time goes in v3:
time: 172 us
  Pallas kernels  169 us (98%)
    pallas_call x1, Pallas kernels, front(): pl.pallas_call(front_kernel, out_shape=(jax.ShapeDtypeStruct((NB, NB), f3...  141 us
    pallas_call x1, Pallas kernels, update(): pl.pallas_call(update_kernel, grid=(NB // UR,), out_shape=(jax.ShapeDtype...  28.4 us

profile of v3, /device:TPU:18, one launch (start us, length us, event | category | flops | bytes accessed | tf_op | source)
XLA Modules:
  0.0 172.1 jit_solution(9844461717201624707)
XLA Ops:
  0.6 1.3 convert_multiply_fusion
  1.9 0.0 copy-start
  1.9 0.8 slice_bitcast_fusion.tsrc
  2.7 141.1 %shard_map.59 = (f32[1024,1024]{1,0:T(8,128)}, f32[1024,512]{1,0:T(8,128)}, f32[2,512,4,4,128]{4,3,2,1,0:T(4,128)}, f32[2,512,128]{2,1,0:T(8,128)}, f32[2,512,128]{2,1,0:T(8,128)}) custom-call(f32[2,512,4,4,128]{4,3,2,1,0:T(4,128)} %bitcast.12, f32[8,128]{1,0:T(8,128)} %bitcast.17, f32[512,128]{1,0:T(8,128)} %slice_bitcast_fusion.tsrc), custom_call_target="tpu_custom_call" | custom-call | tf_op jit(solution)/shard_map/pallas_call | solution.py:480
  143.7 0.0 copy-done
  143.8 28.4 %shard_map.60 = (f32[16384,128]{1,0:T(8,128)}, f32[1024,128]{1,0:T(8,128)}) custom-call(f32[16384,128]{1,0:T(8,128)} %bitcast.13, f32[8,128]{1,0:T(8,128)} %bitcast.18, f32[1024,1024]{1,0:T(8,128)} %get-tuple-element.9.T, f32[16384,128]{1,0:T(8,128)} %bitcast.14, f32[1024,128]{1,0:T(8,128)} %bitcast.16, f32[1024,512]{1,0:T(8,128)} %get-tuple-element.12.X, ...), custom_call_target="tpu_custom_call" | custom-call | tf_op jit(solution)/shard_map/pallas_call | solution.py:564
Async XLA Ops:
  1.9 141.9 %copy-start = (f32[2,1,512,128]{3,2,1,0:T(8,128)}, f32[2,1,512,128]{3,2,1,0:T(8,128)S(1)}, u32[]{:S(2)}) copy-start(f32[2,1,512,128]{3,2,1,0:T(8,128)S(1)} %convert_multiply_fusion) | copy-start | bytes 1572868

commit v4 on v3

--- a/solution.py
+++ b/solution.py
@@ -6,8 +6,6 @@
 from jax.sharding import PartitionSpec as P
 
 MESH = pl.DeviceIdType.MESH
-HIGHEST = lax.Precision.HIGHEST
-HIGH = lax.Precision.HIGH
 PW = 512
 NB = 2 * PW
 BK = 128
@@ -299,15 +297,6 @@
     ]
 
 
-def dot(a, b, dims=((1,), (0,))):
-    return lax.dot_general(a, b, (dims, ((), ())), precision=HIGHEST, preferred_element_type=jnp.float32)
-
-
-def recip(d):
-    r = pltpu.reciprocal(d, approx=True)
-    return r * (2.0 - d * r)
-
-
 def factor128(read, halfway):
     lane = lax.broadcasted_iota(jnp.int32, (8, BK), 1)
     sub = lax.broadcasted_iota(jnp.int32, (8, BK), 0)
@@ -324,7 +313,7 @@
         pivots = None
         for j in range(8):
             d = splat(B[j][j : j + 1, :])
-            inv = recip(d)
+            inv = pltpu.reciprocal(d, approx=True)
             pivots = d if pivots is None else jnp.where(sub == j, d, pivots)
             coef = jnp.where(sub > j, B[j] * inv, 0.0)
             ur, qr = splat(Rp[j : j + 1, :]), splat(Qp[j : j + 1, :])
@@ -355,11 +344,35 @@
     return one(a[0], b[0]) + (one(a[0], b[1]) + one(a[1], b[0]))
 
 
+def less_above(k, line, Uh, Ul, Wh, Wl):
+    for c in range(1, NB // BK):
+
+        @pl.when(k == c)
+        def _():
+            top, here = pl.ds(0, c * BK), pl.ds(c * BK, BK)
+            u = (Uh[top, here], Ul[top, here])
+            for first in range(0, NB, 2 * BK):
+                for hi, lo, start, stop in ((Wh, Wl, 0, c * BK), (Uh, Ul, c * BK, NB)):
+                    start, stop = max(first, start), min(first + 2 * BK, stop)
+                    if start < stop:
+                        to = pl.ds(start, stop - start)
+                        line[:, to] = line[:, to] - dot3(u, (hi[top, to], lo[top, to]), ((0,), (0,)))
+
+
+def finish_row(r0, inverse, line, Uh, Ul, Wh, Wl):
+    rows = pl.ds(r0, BK)
+    whole = dot3(split(inverse[...]), split(line[...]))
+    lane = lax.broadcasted_iota(jnp.int32, (BK, NB), 1)
+    Uh[rows, :], Ul[rows, :] = split(jnp.where(lane >= r0 + BK, whole, 0.0))
+    Wh[rows, :], Wl[rows, :] = split(jnp.where(lane < r0, whole, 0.0))
+    Wh[rows, pl.ds(r0, BK)], Wl[rows, pl.ds(r0, BK)] = split(inverse[...])
+
+
 PRE = 9
 PER = 3
 
 
-def front_kernel(cov, noise, tsrc, t_out, x_out, h_out, g_out, head_out, H, Tg, G, K, E, T, D, Gh, Gl, Wh, Wl, Hd, out_sem, *sems):
+def front_kernel(cov, noise, tsrc, t_out, x_out, h_out, g_out, head_out, H, Tg, G, K, E, T, D, line, Uh, Ul, Gh, Gl, Wh, Wl, Hd, out_sem, *sems):
     spread = Spread(cov, noise, tsrc, H, Tg, G, K, *sems)
     count = NB // BK
 
@@ -372,13 +385,11 @@
 
     K2, G2 = K.reshape(3 * PW * 4, BK), G.reshape(2 * NB * 4, BK)
     spread.start()
-    E[...] = jnp.zeros_like(E)
     slots(0, PRE)
-    lane = lax.broadcasted_iota(jnp.int32, (BK, NB), 1)
+    lane = lax.broadcasted_iota(jnp.int32, (BK, BK), 1)
 
     def step(k, carry):
         r0 = pl.multiple_of(k * BK, BK)
-        rows = pl.ds(r0, BK)
         spread.slot(PRE + PER * k)
 
         @pl.when(k < 4)
@@ -387,37 +398,25 @@
             spread.corner_rows(0, n)
             spread.corner_rows(1, n)
             for s in range(4):
-                to = slice(s * BK, (s + 1) * BK)
-                E[rows, to] = E[rows, to] + jnp.where(lane[:, to] >= r0, K2[pl.ds(n * (BK * 4) + s, BK, stride=4), :], 0.0)
-            for s in range(4):
-                to = slice(PW + s * BK, PW + (s + 1) * BK)
-                E[rows, to] = E[rows, to] + K2[pl.ds((PW + n * BK) * 4 + s, BK, stride=4), :]
+                value = K2[pl.ds(n * (BK * 4) + s, BK, stride=4), :]
+                line[:, s * BK : (s + 1) * BK] = jnp.where(lane + s * BK >= r0, value, 0.0)
+                line[:, PW + s * BK : PW + (s + 1) * BK] = K2[pl.ds((PW + n * BK) * 4 + s, BK, stride=4), :]
 
         @pl.when(k >= 4)
         def _():
             n = jnp.maximum(k - 4, 0)
             spread.corner_rows(2, n)
             for s in range(4):
-                to = slice(PW + s * BK, PW + (s + 1) * BK)
-                E[rows, to] = E[rows, to] + jnp.where(lane[:, to] >= r0, K2[pl.ds((2 * PW + n * BK) * 4 + s, BK, stride=4), :], 0.0)
-
-        W = factor128(lambda p: E[pl.ds(r0 + 8 * p, 8), pl.ds(r0, BK)], lambda: spread.slot(PRE + PER * k + 1))
+                value = K2[pl.ds((2 * PW + n * BK) * 4 + s, BK, stride=4), :]
+                line[:, s * BK : (s + 1) * BK] = jnp.zeros((BK, BK), jnp.float32)
+                line[:, PW + s * BK : PW + (s + 1) * BK] = jnp.where(lane + PW + s * BK >= r0, value, 0.0)
+
+        less_above(k, line, Uh, Ul, Wh, Wl)
+        W = factor128(lambda p: line[8 * p : 8 * p + 8, pl.ds(r0, BK)], lambda: spread.slot(PRE + PER * k + 1))
         for p in range(16):
             D[pl.ds(8 * p, 8), :] = W[p]
         spread.slot(PRE + PER * k + 2)
-        E[rows, :] = dot(D[...], E[rows, :])
-        E[rows, pl.ds(r0, BK)] = D[...]
-        hi, lo = split(jnp.where(lane < r0 + BK, E[rows, :], 0.0))
-        Wh[rows, :] = hi
-        Wl[rows, :] = lo
-
-        def under(i, carry):
-            i0 = pl.multiple_of(i * BK, BK)
-            E[pl.ds(i0, BK), pl.ds(r0, BK)] = jnp.zeros((BK, BK), jnp.float32)
-            E[pl.ds(i0, BK), :] = E[pl.ds(i0, BK), :] - dot(E[rows, pl.ds(i0, BK)], E[rows, :], ((0,), (0,)))
-            return carry
-
-        lax.fori_loop(k + 1, count, under, 0)
+        finish_row(r0, D, line, Uh, Ul, Wh, Wl)
         return carry
 
     lax.fori_loop(0, count, step, 0)
@@ -500,6 +499,9 @@
             pltpu.VMEM((NB, NB), f32),
             pltpu.VMEM((NB, NB), f32),
             pltpu.VMEM((BK, BK), f32),
+            pltpu.VMEM((BK, NB), f32),
+            pltpu.VMEM((NB, NB), bf16),
+            pltpu.VMEM((NB, NB), bf16),
             pltpu.VMEM((PW // 2, NB), bf16),
             pltpu.VMEM((PW // 2, NB), bf16),
             pltpu.VMEM((NB, NB), bf16),

time: 172 us -> 160 us (0.930)
  Pallas kernels: 169 us -> 157 us
    pallas_call x1, Pallas kernels: 141 us -> 128 us  [front(): pl.pallas_call(front_kernel, out_shape=(jax.ShapeDtypeStruct((NB, NB), f3...]
where the time goes in v4:
time: 160 us
  Pallas kernels  157 us (98%)
    pallas_call x1, Pallas kernels, front(): pl.pallas_call(front_kernel, out_shape=(jax.ShapeDtypeStruct((NB, NB), f3...  128 us
    pallas_call x1, Pallas kernels, update(): pl.pallas_call(update_kernel, grid=(NB // UR,), out_shape=(jax.ShapeDtype...  28.4 us

profile of v4, /device:TPU:18, one launch (start us, length us, event | category | flops | bytes accessed | tf_op | source)
XLA Modules:
  0.0 159.5 jit_solution(5421074311533601946)
XLA Ops:
  0.6 1.3 convert_multiply_fusion
  1.9 0.0 copy-start
  1.9 0.8 slice_bitcast_fusion.tsrc
  2.7 128.4 %shard_map.59 = (f32[1024,1024]{1,0:T(8,128)}, f32[1024,512]{1,0:T(8,128)}, f32[2,512,4,4,128]{4,3,2,1,0:T(4,128)}, f32[2,512,128]{2,1,0:T(8,128)}, f32[2,512,128]{2,1,0:T(8,128)}) custom-call(f32[2,512,4,4,128]{4,3,2,1,0:T(4,128)} %bitcast.12, f32[8,128]{1,0:T(8,128)} %bitcast.17, f32[512,128]{1,0:T(8,128)} %slice_bitcast_fusion.tsrc), custom_call_target="tpu_custom_call" | custom-call | tf_op jit(solution)/shard_map/pallas_call | solution.py:479
  131.1 0.0 copy-done
  131.1 28.4 %shard_map.60 = (f32[16384,128]{1,0:T(8,128)}, f32[1024,128]{1,0:T(8,128)}) custom-call(f32[16384,128]{1,0:T(8,128)} %bitcast.13, f32[8,128]{1,0:T(8,128)} %bitcast.18, f32[1024,1024]{1,0:T(8,128)} %get-tuple-element.9.T, f32[16384,128]{1,0:T(8,128)} %bitcast.14, f32[1024,128]{1,0:T(8,128)} %bitcast.16, f32[1024,512]{1,0:T(8,128)} %get-tuple-element.12.X, ...), custom_call_target="tpu_custom_call" | custom-call | tf_op jit(solution)/shard_map/pallas_call | solution.py:566
Async XLA Ops:
  1.9 129.2 %copy-start = (f32[2,1,512,128]{3,2,1,0:T(8,128)}, f32[2,1,512,128]{3,2,1,0:T(8,128)S(1)}, u32[]{:S(2)}) copy-start(f32[2,1,512,128]{3,2,1,0:T(8,128)S(1)} %convert_multiply_fusion) | copy-start | bytes 1572868

commit v5 on v4

--- a/solution.py
+++ b/solution.py
@@ -38,8 +38,8 @@
 
 
 class Spread:
-    LATE = (0, 4)
-    GLATE = 9
+    LATE = (0, 1)
+    GLATE = 8
 
     def __init__(self, cov, noise, tsrc, H, Tg, G, K, own, hr, hs, tr, ts, kr, ks, gr, gs):
         self.cov, self.noise, self.tsrc, self.own = cov, noise, tsrc, own
@@ -142,7 +142,7 @@
         for root in range(2):
             for tree in range(4):
                 depth, late = self.depth[root][tree], s - self.LATE[root]
-                self.h_slot(root, tree, jnp.where(late - depth < 4, late - depth, jnp.where(late - 2 * depth < 4, -1, late - 2 * depth)))
+                self.h_slot(root, tree, jnp.where(late - depth < 4, late - depth, jnp.where(late - 3 * depth < 4, -1, late - 3 * depth)))
         for block in range(3):
             for tree in range(4):
                 root, way = block // 2, tree % 2

time: 160 us -> 158 us (0.988)
  Pallas kernels: 157 us -> 155 us
where the time goes in v5:
time: 158 us
  Pallas kernels  155 us (98%)
    pallas_call x1, Pallas kernels, front(): pl.pallas_call(front_kernel, out_shape=(jax.ShapeDtypeStruct((NB, NB), f3...  127 us
    pallas_call x1, Pallas kernels, update(): pl.pallas_call(update_kernel, grid=(NB // UR,), out_shape=(jax.ShapeDtype...  28.4 us

profile of v5, /device:TPU:18, one launch (start us, length us, event | category | flops | bytes accessed | tf_op | source)
XLA Modules:
  0.0 157.9 jit_solution(6478325278170413271)
XLA Ops:
  0.6 1.3 convert_multiply_fusion
  1.9 0.0 copy-start
  1.9 0.8 slice_bitcast_fusion.tsrc
  2.7 126.8 %shard_map.59 = (f32[1024,1024]{1,0:T(8,128)}, f32[1024,512]{1,0:T(8,128)}, f32[2,512,4,4,128]{4,3,2,1,0:T(4,128)}, f32[2,512,128]{2,1,0:T(8,128)}, f32[2,512,128]{2,1,0:T(8,128)}) custom-call(f32[2,512,4,4,128]{4,3,2,1,0:T(4,128)} %bitcast.12, f32[8,128]{1,0:T(8,128)} %bitcast.17, f32[512,128]{1,0:T(8,128)} %slice_bitcast_fusion.tsrc), custom_call_target="tpu_custom_call" | custom-call | tf_op jit(solution)/shard_map/pallas_call | solution.py:479
  129.5 0.0 copy-done
  129.5 28.4 %shard_map.60 = (f32[16384,128]{1,0:T(8,128)}, f32[1024,128]{1,0:T(8,128)}) custom-call(f32[16384,128]{1,0:T(8,128)} %bitcast.13, f32[8,128]{1,0:T(8,128)} %bitcast.18, f32[1024,1024]{1,0:T(8,128)} %get-tuple-element.9.T, f32[16384,128]{1,0:T(8,128)} %bitcast.14, f32[1024,128]{1,0:T(8,128)} %bitcast.16, f32[1024,512]{1,0:T(8,128)} %get-tuple-element.12.X, ...), custom_call_target="tpu_custom_call" | custom-call | tf_op jit(solution)/shard_map/pallas_call | solution.py:566
Async XLA Ops:
  1.9 127.6 %copy-start = (f32[2,1,512,128]{3,2,1,0:T(8,128)}, f32[2,1,512,128]{3,2,1,0:T(8,128)S(1)}, u32[]{:S(2)}) copy-start(f32[2,1,512,128]{3,2,1,0:T(8,128)S(1)} %convert_multiply_fusion) | copy-start | bytes 1572868
